TPU v7x, 512 devices: a whole 4x8x8 slice. The times are simulated.
512 devices in a mesh: seq: 128 (over y, z, core), tp: 4 (over x).
Axes of the slice: x: 4, y: 8, z: 8, core: 2. Of those that a mesh axis runs over, the one named last changes fastest.
Arguments:
- proj: bfloat16 [3, 512, 16384], P(None, 'tp', 'seq'), may hold values from -6 to 6
- short_filter: float32 [3, 512, 3], P(None, 'tp'), may hold values from -3.5 to 3.5
- skip_gain: float32 [512], P('tp'), may hold values from -4 to 4
- norm_gain: float32 [512], P('tp'), may hold values from 0.5 to 1.5
- filter_spectrum: float32 [2, 512, 32768], P(None, 'tp', 'seq'), may hold values from -30 to 30, as said below
Outputs:
- output: bfloat16 [512, 16384], P('tp', 'seq')
Inputs may be any that keep to these rules, and one draw needn't show every extreme that they name: `filter_spectrum`: real and imaginary parts of a complex filter's transform, of order one to a few, with no symmetry between frequencies k and 32768 - k.
All inputs are finite; a program needn't handle non-finite values.
Results may differ from a plain program's by a relative error of at most 0.008.
Values may be sent and summed in bfloat16 or wider, within the bound.
No kernel may reach another device: no remote copies, remote signals or barrier semaphores. Data moves between devices by JAX's collectives and lax.ppermute only.
A program may use at most 64 MiB of HBM per device.

v0:
```python
import math

import jax
import jax.numpy as jnp
from jax import lax
from jax.sharding import PartitionSpec as P

HIGH = lax.Precision.HIGHEST


def shifted(block, axis, distance):
    devices = range(lax.axis_size(axis))
    route = [(i - distance, i) for i in devices if i - distance in devices]
    return lax.ppermute(block, axis, route)


def table(row_index, col_index, length, sign):
    angle_int = row_index[:, None] * col_index[None, :] % length
    angle = angle_int.astype(jnp.float32) * (2.0 * math.pi / length)
    return (jnp.cos(angle), sign * jnp.sin(angle))


def complex_dot(form, real_part, imag_part, tab_real, tab_imag):
    out_real = jnp.einsum(form, real_part, tab_real, precision=HIGH) - jnp.einsum(
        form, imag_part, tab_imag, precision=HIGH
    )
    out_imag = jnp.einsum(form, real_part, tab_imag, precision=HIGH) + jnp.einsum(
        form, imag_part, tab_real, precision=HIGH
    )
    return (out_real, out_imag)


def complex_mul(a_real, a_imag, b_real, b_imag):
    return (a_real * b_real - a_imag * b_imag, a_real * b_imag + a_imag * b_real)


def per_device(proj, short_filter, skip_gain, norm_gain, filter_spectrum):
    chans = proj.shape[1]
    tok = proj.shape[2]
    peers = lax.axis_size("seq")
    me_seq = lax.axis_index("seq")
    block = tok // peers
    total = 2 * tok * peers
    inner = tok // 128
    outer = 128
    prev = shifted(proj[:, :, tok - 2 :], "seq", 1)
    wide = jnp.concatenate([prev, proj], axis=2).astype(jnp.float32)
    conv = (
        short_filter[:, :, 0:1] * wide[:, :, 2:]
        + short_filter[:, :, 1:2] * wide[:, :, 1 : tok + 1]
        + short_filter[:, :, 2:3] * wide[:, :, 0:tok]
    )
    query, keyed, value = (conv[0], conv[1], conv[2])
    mixed = (keyed * value).astype(jnp.bfloat16)
    columns = lax.all_to_all(
        mixed.reshape(chans, peers, block), "seq", split_axis=1, concat_axis=1, tiled=True
    ).astype(jnp.float32)
    coarse_c, coarse_s = table(
        jnp.arange(peers, dtype=jnp.int32), jnp.arange(2 * peers, dtype=jnp.int32), 2 * peers, -1.0
    )
    first_re = jnp.einsum("csb,sk->ckb", columns, coarse_c, precision=HIGH)
    first_im = jnp.einsum("csb,sk->ckb", columns, coarse_s, precision=HIGH)
    positions = me_seq * block + jnp.arange(block, dtype=jnp.int32)
    twist_c, twist_s = table(jnp.arange(2 * peers, dtype=jnp.int32), positions, total, -1.0)
    first_re, first_im = complex_mul(first_re, first_im, twist_c[None], twist_s[None])
    rows_re, rows_im = (
        lax.all_to_all(
            first_re.reshape(chans, peers, 2, block), "seq", split_axis=1, concat_axis=3, tiled=True
        ),
        lax.all_to_all(
            first_im.reshape(chans, peers, 2, block), "seq", split_axis=1, concat_axis=3, tiled=True
        ),
    )
    rows_re = rows_re.reshape(chans, 2, outer, inner)
    rows_im = rows_im.reshape(chans, 2, outer, inner)
    outer_c, outer_s = table(
        jnp.arange(outer, dtype=jnp.int32), jnp.arange(outer, dtype=jnp.int32), outer, -1.0
    )
    part_re, part_im = complex_dot("crba,bk->crka", rows_re, rows_im, outer_c, outer_s)
    local_c, local_s = table(
        jnp.arange(outer, dtype=jnp.int32), jnp.arange(inner, dtype=jnp.int32), tok, -1.0
    )
    part_re, part_im = complex_mul(part_re, part_im, local_c[None, None], local_s[None, None])
    inner_c, inner_s = table(
        jnp.arange(inner, dtype=jnp.int32), jnp.arange(inner, dtype=jnp.int32), inner, -1.0
    )
    spec_re, spec_im = complex_dot("crka,am->crkm", part_re, part_im, inner_c, inner_s)
    flat_re = jnp.transpose(spec_re, (0, 1, 3, 2)).reshape(chans, 2, peers, block)
    flat_im = jnp.transpose(spec_im, (0, 1, 3, 2)).reshape(chans, 2, peers, block)
    nat_re, nat_im = (
        lax.all_to_all(flat_re, "seq", split_axis=2, concat_axis=1, tiled=True),
        lax.all_to_all(flat_im, "seq", split_axis=2, concat_axis=1, tiled=True),
    )
    nat_re = jnp.transpose(nat_re.reshape(chans, 2 * peers, block), (0, 2, 1)).reshape(
        chans, 2 * tok
    )
    nat_im = jnp.transpose(nat_im.reshape(chans, 2 * peers, block), (0, 2, 1)).reshape(
        chans, 2 * tok
    )
    nat_re, nat_im = complex_mul(nat_re, nat_im, filter_spectrum[0], filter_spectrum[1])
    send_re = jnp.transpose(nat_re.reshape(chans, block, 2 * peers), (0, 2, 1)).reshape(
        chans, peers, 2, block
    )
    send_im = jnp.transpose(nat_im.reshape(chans, block, 2 * peers), (0, 2, 1)).reshape(
        chans, peers, 2, block
    )
    back_re, back_im = (
        lax.all_to_all(send_re, "seq", split_axis=1, concat_axis=3, tiled=True),
        lax.all_to_all(send_im, "seq", split_axis=1, concat_axis=3, tiled=True),
    )
    prod_re = jnp.transpose(back_re.reshape(chans, 2, inner, outer), (0, 1, 3, 2))
    prod_im = jnp.transpose(back_im.reshape(chans, 2, inner, outer), (0, 1, 3, 2))
    inv_inner_c, inv_inner_s = table(
        jnp.arange(inner, dtype=jnp.int32), jnp.arange(inner, dtype=jnp.int32), inner, 1.0
    )
    back_re, back_im = complex_dot("crkm,ma->crka", prod_re, prod_im, inv_inner_c, inv_inner_s)
    back_re, back_im = complex_mul(back_re, back_im, local_c[None, None], -local_s[None, None])
    inv_outer_c, inv_outer_s = table(
        jnp.arange(outer, dtype=jnp.int32), jnp.arange(outer, dtype=jnp.int32), outer, 1.0
    )
    time_re, time_im = complex_dot("crka,kb->crba", back_re, back_im, inv_outer_c, inv_outer_s)
    time_re = time_re.reshape(chans, 2, tok)
    time_im = time_im.reshape(chans, 2, tok)
    coarse_rows = 2 * me_seq + jnp.arange(2, dtype=jnp.int32)
    back_c, back_s = table(coarse_rows, jnp.arange(tok, dtype=jnp.int32), total, 1.0)
    time_re, time_im = complex_mul(time_re, time_im, back_c[None], back_s[None])
    gath_re, gath_im = (
        lax.all_to_all(
            time_re.reshape(chans, 2, peers, block), "seq", split_axis=2, concat_axis=1, tiled=True
        ),
        lax.all_to_all(
            time_im.reshape(chans, 2, peers, block), "seq", split_axis=2, concat_axis=1, tiled=True
        ),
    )
    gath_re = gath_re.reshape(chans, 2 * peers, block)
    gath_im = gath_im.reshape(chans, 2 * peers, block)
    final_c, final_s = table(
        jnp.arange(2 * peers, dtype=jnp.int32), jnp.arange(peers, dtype=jnp.int32), 2 * peers, 1.0
    )
    shard_out = (
        jnp.einsum("ckb,ks->csb", gath_re, final_c, precision=HIGH)
        - jnp.einsum("ckb,ks->csb", gath_im, final_s, precision=HIGH)
    ) / total
    long_out = lax.all_to_all(shard_out, "seq", split_axis=1, concat_axis=2, tiled=True).reshape(
        chans, tok
    )
    pre = query * (long_out + skip_gain[:, None] * mixed.astype(jnp.float32))
    groups = lax.axis_size("tp")
    meansq = lax.psum(jnp.sum(pre * pre, axis=0), "tp") / (chans * groups)
    return (pre * lax.rsqrt(meansq + 1e-05)[None, :] * norm_gain[:, None]).astype(jnp.bfloat16)


def solution(mesh):
    return jax.shard_map(
        per_device,
        mesh=mesh,
        in_specs=(
            P(None, "tp", "seq"),
            P(None, "tp", None),
            P("tp"),
            P("tp"),
            P(None, "tp", "seq"),
        ),
        out_specs=P("tp", "seq"),
        check_vma=False,
    )
```

profile of v0, /device:TPU:1, one launch (start us, length us, event | category | flops | bytes accessed | tf_op | source)
XLA Modules:
  0.0 223.2 jit_solution(13435600940727760326)
XLA Ops:
  0.0 1.1 slice.37
  1.1 5.4 %collective-permute-start = (bf16[3,128,2]{2,1,0:T(8,128)(2,1)S(1)}, bf16[3,128,2]{2,1,0:T(8,128)(2,1)S(1)}, u32[]{:S(2)}, u32[]{:S(2)}) collective-permute-start(bf16[3,128,2]{2,1,0:T(8,128)(2,1)S(1)} %slice.37), channel_id=1, source_target_pairs={{0,4},{4,8},{8,12},{12,16},{16,20},{20,24},{24,28},{28,32},{32,36}... | collective-permute-start | bytes 4616 | tf_op jit(solution)/shard_map/ppermute | solution.py:14
  6.5 3.5 %collective-permute-done = bf16[3,128,2]{2,1,0:T(8,128)(2,1)S(1)} collective-permute-done((bf16[3,128,2]{2,1,0:T(8,128)(2,1)S(1)}, bf16[3,128,2]{2,1,0:T(8,128)(2,1)S(1)}, u32[]{:S(2)}, u32[]{:S(2)}) %collective-permute-start) | collective-permute-done | bytes 1568 | tf_op jit(solution)/shard_map/ppermute | solution.py:14
  11.3 16.6 %all-to-all-start = ((bf16[128,128,1]{0,2,1:T(2,128)(2,1)}), bf16[128,128,1]{0,2,1:T(2,128)(2,1)S(1)}, u32[]{:S(2)}, u32[]{:S(2)}) async-start(bf16[128,128,1]{0,2,1:T(2,128)(2,1)} %copy.72), calls=%async_computation | async-start | bytes 131072 | tf_op jit(solution)/shard_map/all_to_all | solution.py:55
  27.9 11.4 %all-to-all-done = bf16[128,128,1]{0,2,1:T(2,128)(2,1)S(1)} async-done(((bf16[128,128,1]{0,2,1:T(2,128)(2,1)}), bf16[128,128,1]{0,2,1:T(2,128)(2,1)S(1)}, u32[]{:S(2)}, u32[]{:S(2)}) %all-to-all-start) | async-done | bytes 32800 | tf_op jit(solution)/shard_map/all_to_all | solution.py:55
  40.2 1.4 multiply_add_fusion.3
  41.6 17.7 %all_to_all.134 = f32[128,128,2,1]{0,2,3,1:T(2,128)S(1)} all-to-all(f32[128,128,2,1]{0,2,3,1:T(2,128)S(1)} %bitcast.201), channel_id=1, replica_groups=mesh['seq'=128,'tp'=4] {'seq'}, dimensions={1} | all-to-all | bytes 262144 | tf_op jit(solution)/shard_map/all_to_all | solution.py:67
  59.3 5.9 %all-to-all-start.2 = ((f32[128,128,2,1]{0,2,3,1:T(2,128)}), f32[128,128,2,1]{0,2,3,1:T(2,128)S(1)}, u32[]{:S(2)}, u32[]{:S(2)}) async-start(f32[128,128,2,1]{0,2,3,1:T(2,128)} %bitcast.15), calls=%async_computation.2 | async-start | bytes 262144 | tf_op jit(solution)/shard_map/all_to_all | solution.py:70
  66.3 11.2 %all-to-all-done.2 = f32[128,128,2,1]{0,2,3,1:T(2,128)S(1)} async-done(((f32[128,128,2,1]{0,2,3,1:T(2,128)}), f32[128,128,2,1]{0,2,3,1:T(2,128)S(1)}, u32[]{:S(2)}, u32[]{:S(2)}) %all-to-all-start.2) | async-done | bytes 131104 | tf_op jit(solution)/shard_map/all_to_all | solution.py:70
  79.4 6.3 %all-to-all-start.3 = ((f32[128,2,128,1]{0,1,3,2:T(2,128)}), f32[128,2,128,1]{0,1,3,2:T(2,128)S(1)}, u32[]{:S(2)}, u32[]{:S(2)}) async-start(f32[128,2,128,1]{0,1,3,2:T(2,128)} %copy.78), calls=%async_computation.3 | async-start | bytes 262144 | tf_op jit(solution)/shard_map/all_to_all | solution.py:91
  86.5 11.5 %all-to-all-done.3 = f32[128,2,128,1]{0,1,3,2:T(2,128)S(1)} async-done(((f32[128,2,128,1]{0,1,3,2:T(2,128)}), f32[128,2,128,1]{0,1,3,2:T(2,128)S(1)}, u32[]{:S(2)}, u32[]{:S(2)}) %all-to-all-start.3) | async-done | bytes 131104 | tf_op jit(solution)/shard_map/all_to_all | solution.py:91
  98.0 6.2 %all-to-all-start.4 = ((f32[128,2,128,1]{0,1,3,2:T(2,128)}), f32[128,2,128,1]{0,1,3,2:T(2,128)S(1)}, u32[]{:S(2)}, u32[]{:S(2)}) async-start(f32[128,2,128,1]{0,1,3,2:T(2,128)} %copy.80), calls=%async_computation.4 | async-start | bytes 262144 | tf_op jit(solution)/shard_map/all_to_all | solution.py:92
  104.5 12.1 %all-to-all-done.4 = f32[128,2,128,1]{0,1,3,2:T(2,128)S(1)} async-done(((f32[128,2,128,1]{0,1,3,2:T(2,128)}), f32[128,2,128,1]{0,1,3,2:T(2,128)S(1)}, u32[]{:S(2)}, u32[]{:S(2)}) %all-to-all-start.4) | async-done | bytes 131104 | tf_op jit(solution)/shard_map/all_to_all | solution.py:92
  117.4 6.2 %all-to-all-start.5 = ((f32[128,128,2,1]{0,2,3,1:T(2,128)}), f32[128,128,2,1]{0,2,3,1:T(2,128)S(1)}, u32[]{:S(2)}, u32[]{:S(2)}) async-start(f32[128,128,2,1]{0,2,3,1:T(2,128)} %get-tuple-element.5), calls=%async_computation.5 | async-start | bytes 262144 | tf_op jit(solution)/shard_map/all_to_all | solution.py:108
  123.6 12.3 %all-to-all-done.5 = f32[128,128,2,1]{0,2,3,1:T(2,128)S(1)} async-done(((f32[128,128,2,1]{0,2,3,1:T(2,128)}), f32[128,128,2,1]{0,2,3,1:T(2,128)S(1)}, u32[]{:S(2)}, u32[]{:S(2)}) %all-to-all-start.5) | async-done | bytes 131104 | tf_op jit(solution)/shard_map/all_to_all | solution.py:108
  135.9 6.2 %all-to-all-start.6 = ((f32[128,128,2,1]{0,2,3,1:T(2,128)}), f32[128,128,2,1]{0,2,3,1:T(2,128)S(1)}, u32[]{:S(2)}, u32[]{:S(2)}) async-start(f32[128,128,2,1]{0,2,3,1:T(2,128)} %get-tuple-element.6), calls=%async_computation.6 | async-start | bytes 262144 | tf_op jit(solution)/shard_map/all_to_all | solution.py:109
  142.3 12.0 %all-to-all-done.6 = f32[128,128,2,1]{0,2,3,1:T(2,128)S(1)} async-done(((f32[128,128,2,1]{0,2,3,1:T(2,128)}), f32[128,128,2,1]{0,2,3,1:T(2,128)S(1)}, u32[]{:S(2)}, u32[]{:S(2)}) %all-to-all-start.6) | async-done | bytes 131104 | tf_op jit(solution)/shard_map/all_to_all | solution.py:109
  157.3 6.2 %all-to-all-start.7 = ((f32[128,2,128,1]{0,1,3,2:T(2,128)}), f32[128,2,128,1]{0,1,3,2:T(2,128)S(1)}, u32[]{:S(2)}, u32[]{:S(2)}) async-start(f32[128,2,128,1]{0,1,3,2:T(2,128)} %copy.86), calls=%async_computation.7 | async-start | bytes 262144 | tf_op jit(solution)/shard_map/all_to_all | solution.py:128
  164.3 11.6 %all-to-all-done.7 = f32[128,2,128,1]{0,1,3,2:T(2,128)S(1)} async-done(((f32[128,2,128,1]{0,1,3,2:T(2,128)}), f32[128,2,128,1]{0,1,3,2:T(2,128)S(1)}, u32[]{:S(2)}, u32[]{:S(2)}) %all-to-all-start.7) | async-done | bytes 131104 | tf_op jit(solution)/shard_map/all_to_all | solution.py:128
  175.8 6.4 %all-to-all-start.8 = ((f32[128,2,128,1]{0,1,3,2:T(2,128)}), f32[128,2,128,1]{0,1,3,2:T(2,128)S(1)}, u32[]{:S(2)}, u32[]{:S(2)}) async-start(f32[128,2,128,1]{0,1,3,2:T(2,128)} %copy.87), calls=%async_computation.8 | async-start | bytes 262144 | tf_op jit(solution)/shard_map/all_to_all | solution.py:131
  183.1 11.4 %all-to-all-done.8 = f32[128,2,128,1]{0,1,3,2:T(2,128)S(1)} async-done(((f32[128,2,128,1]{0,1,3,2:T(2,128)}), f32[128,2,128,1]{0,1,3,2:T(2,128)S(1)}, u32[]{:S(2)}, u32[]{:S(2)}) %all-to-all-start.8) | async-done | bytes 131104 | tf_op jit(solution)/shard_map/all_to_all | solution.py:131
  194.5 0.9 fusion.4
  195.3 17.3 %all_to_all.135 = f32[128,128,1]{0,2,1:T(1,128)S(1)} all-to-all(f32[128,128,1]{0,2,1:T(1,128)S(1)} %bitcast.202), channel_id=1, replica_groups=mesh['seq'=128,'tp'=4] {'seq'}, dimensions={1} | all-to-all | bytes 131072 | tf_op jit(solution)/shard_map/all_to_all | solution.py:144
  213.4 8.5 %psum.7 = f32[128]{0:T(128)S(1)} all-reduce(f32[128]{0:T(128)S(1)} %multiply_reduce_fusion), channel_id=1, replica_groups=mesh['seq'=128,'tp'=4] {'tp'}, use_global_device_ids=true, to_apply=%region_1.2 | all-reduce | flops 128 | bytes 1024 | tf_op jit(solution)/shard_map/psum | solution.py:149
  (48 shorter events, 13.8 us)
Async XLA Ops:
  0.0 10.0 %copy-start = (bf16[3,128,128]{2,1,0:T(8,128)(2,1)S(1)}, bf16[3,128,128]{2,1,0:T(8,128)(2,1)}, u32[]{:S(2)}) copy-start(bf16[3,128,128]{2,1,0:T(8,128)(2,1)} %param.5) | copy-start | bytes 294916
  0.0 6.5 %copy-start.2 = (f32[3,128,3]{1,2,0:T(4,128)S(1)}, f32[3,128,3]{1,2,0:T(4,128)}, u32[]{:S(2)}) copy-start(f32[3,128,3]{1,2,0:T(4,128)} %param.6) | copy-start | bytes 13828
  1.1 8.9 %collective-permute-start = (bf16[3,128,2]{2,1,0:T(8,128)(2,1)S(1)}, bf16[3,128,2]{2,1,0:T(8,128)(2,1)S(1)}, u32[]{:S(2)}, u32[]{:S(2)}) collective-permute-start(bf16[3,128,2]{2,1,0:T(8,128)(2,1)S(1)} %slice.37), channel_id=1, source_target_pairs={{0,4},{4,8},{8,12},{12,16},{16,20},{20,24},{24,28},{28,32},{32,36}... | collective-permute-start | bytes 4616 | tf_op jit(solution)/shard_map/ppermute | solution.py:14
  11.3 28.1 %all-to-all-start = ((bf16[128,128,1]{0,2,1:T(2,128)(2,1)}), bf16[128,128,1]{0,2,1:T(2,128)(2,1)S(1)}, u32[]{:S(2)}, u32[]{:S(2)}) async-start(bf16[128,128,1]{0,2,1:T(2,128)(2,1)} %copy.72), calls=%async_computation | async-start | bytes 131072 | tf_op jit(solution)/shard_map/all_to_all | solution.py:55
  59.3 18.2 %all-to-all-start.2 = ((f32[128,128,2,1]{0,2,3,1:T(2,128)}), f32[128,128,2,1]{0,2,3,1:T(2,128)S(1)}, u32[]{:S(2)}, u32[]{:S(2)}) async-start(f32[128,128,2,1]{0,2,3,1:T(2,128)} %bitcast.15), calls=%async_computation.2 | async-start | bytes 262144 | tf_op jit(solution)/shard_map/all_to_all | solution.py:70
  79.4 18.6 %all-to-all-start.3 = ((f32[128,2,128,1]{0,1,3,2:T(2,128)}), f32[128,2,128,1]{0,1,3,2:T(2,128)S(1)}, u32[]{:S(2)}, u32[]{:S(2)}) async-start(f32[128,2,128,1]{0,1,3,2:T(2,128)} %copy.78), calls=%async_computation.3 | async-start | bytes 262144 | tf_op jit(solution)/shard_map/all_to_all | solution.py:91
  85.7 18.5 %copy-start.1 = (f32[2,128,256]{2,1,0:T(8,128)S(1)}, f32[2,128,256]{2,1,0:T(8,128)}, u32[]{:S(2)}) copy-start(f32[2,128,256]{2,1,0:T(8,128)} %param.9) | copy-start | bytes 786436
  98.0 18.6 %all-to-all-start.4 = ((f32[128,2,128,1]{0,1,3,2:T(2,128)}), f32[128,2,128,1]{0,1,3,2:T(2,128)S(1)}, u32[]{:S(2)}, u32[]{:S(2)}) async-start(f32[128,2,128,1]{0,1,3,2:T(2,128)} %copy.80), calls=%async_computation.4 | async-start | bytes 262144 | tf_op jit(solution)/shard_map/all_to_all | solution.py:92
  117.4 18.5 %all-to-all-start.5 = ((f32[128,128,2,1]{0,2,3,1:T(2,128)}), f32[128,128,2,1]{0,2,3,1:T(2,128)S(1)}, u32[]{:S(2)}, u32[]{:S(2)}) async-start(f32[128,128,2,1]{0,2,3,1:T(2,128)} %get-tuple-element.5), calls=%async_computation.5 | async-start | bytes 262144 | tf_op jit(solution)/shard_map/all_to_all | solution.py:108
  135.9 18.4 %all-to-all-start.6 = ((f32[128,128,2,1]{0,2,3,1:T(2,128)}), f32[128,128,2,1]{0,2,3,1:T(2,128)S(1)}, u32[]{:S(2)}, u32[]{:S(2)}) async-start(f32[128,128,2,1]{0,2,3,1:T(2,128)} %get-tuple-element.6), calls=%async_computation.6 | async-start | bytes 262144 | tf_op jit(solution)/shard_map/all_to_all | solution.py:109
  157.3 18.6 %all-to-all-start.7 = ((f32[128,2,128,1]{0,1,3,2:T(2,128)}), f32[128,2,128,1]{0,1,3,2:T(2,128)S(1)}, u32[]{:S(2)}, u32[]{:S(2)}) async-start(f32[128,2,128,1]{0,1,3,2:T(2,128)} %copy.86), calls=%async_computation.7 | async-start | bytes 262144 | tf_op jit(solution)/shard_map/all_to_all | solution.py:128
  175.8 18.6 %all-to-all-start.8 = ((f32[128,2,128,1]{0,1,3,2:T(2,128)}), f32[128,2,128,1]{0,1,3,2:T(2,128)S(1)}, u32[]{:S(2)}, u32[]{:S(2)}) async-start(f32[128,2,128,1]{0,1,3,2:T(2,128)} %copy.87), calls=%async_computation.8 | async-start | bytes 262144 | tf_op jit(solution)/shard_map/all_to_all | solution.py:131
  212.6 0.7 copy-start.3
  221.9 0.7 copy-start.4
where the time goes:
time: 224 us; the launch traced here: 223 us
  waiting for transfers between devices  96.9 us (43%)
  starting transfers between devices  65.4 us (29%)
  blocking collectives  43.4 us (19%)
  matrix products  8.01 us (4%)
  local copies, waits for them, and re-layouts  6.84 us (3%)
  other arithmetic  2.32 us (1%)
    all_to_all x1, blocking collectives, per_device(): lax.all_to_all(first_re.reshape(chans, peers, 2, block), 'seq', split_axi...  17.7 us
    all_to_all x1, blocking collectives, per_device(): lax.all_to_all(shard_out, 'seq', split_axis=1, concat_axis=2, tiled=True)  17.3 us
    all_to_all x1, starting transfers between devices, per_device(): lax.all_to_all(mixed.reshape(chans, peers, block), 'seq', split_axis=1, c...  16.6 us
    all_to_all x1, waiting for transfers between devices, per_device(): lax.all_to_all(send_re, 'seq', split_axis=1, concat_axis=3, tiled=True)  12.3 us
    all_to_all x1, waiting for transfers between devices, per_device(): lax.all_to_all(flat_im, 'seq', split_axis=2, concat_axis=1, tiled=True)  12.1 us
    all_to_all x1, waiting for transfers between devices, per_device(): lax.all_to_all(send_im, 'seq', split_axis=1, concat_axis=3, tiled=True)  12 us
    all_to_all x1, waiting for transfers between devices, per_device(): lax.all_to_all(time_re.reshape(chans, 2, peers, block), 'seq', split_axis...  11.6 us
    all_to_all x1, waiting for transfers between devices, per_device(): lax.all_to_all(flat_re, 'seq', split_axis=2, concat_axis=1, tiled=True)  11.5 us
  transfers between devices with their start and end apart: 9, of which 9 were waited for; matrix products, arithmetic and copies ran while one was open for 2% of the time, Pallas kernels for 0%

commit v1 on v0

v1 whole, which is shorter than its diff:
```python
import functools

import jax
import jax.numpy as jnp
import numpy as np
from jax import lax
from jax.experimental import pallas as pl
from jax.experimental.pallas import tpu as pltpu
from jax.sharding import PartitionSpec as P

ROWS = 8


def tables(n_coarse, n_fine):
    total = 2 * n_coarse * n_fine
    n1 = np.arange(n_coarse)
    k1 = np.arange(2 * n_coarse)
    n2 = np.arange(n_fine)
    first = 2.0 * np.pi * (np.outer(n1, k1) % (2 * n_coarse)) / (2 * n_coarse)
    edge = np.concatenate([np.cos(first), -np.sin(first)], axis=1)
    inner = 2.0 * np.pi * (np.outer(n2, n2) % n_fine) / n_fine
    w_re, w_im = np.cos(inner), -np.sin(inner)
    fwd = np.block([[w_re, -w_im], [w_im, w_re]])
    inv = np.block([[w_re, w_im], [-w_im, w_re]])
    turn = 2.0 * np.pi * (np.outer(n2, k1) % total) / total
    bf16 = functools.partial(jnp.asarray, dtype=jnp.bfloat16)
    f32 = functools.partial(jnp.asarray, dtype=jnp.float32)
    return bf16(edge), bf16(fwd), bf16(inv), f32(np.cos(turn)), f32(-np.sin(turn))


def pack_kernel(proj_ref, filt_ref, out_ref, wide):
    chans = proj_ref.shape[1]
    lanes = proj_ref.shape[2]
    row = lambda r: pl.ds(r, chans, stride=ROWS)
    for i in range(3):
        wide[row(i), :] = proj_ref[i].astype(jnp.float32)
    for part in range(2):
        for half in range(2):
            wide[row(3 + 2 * part + half), :] = filt_ref[part, :, lanes * half : lanes * (half + 1)]
    wide[row(7), :] = jnp.zeros((chans, lanes), jnp.float32)
    out_ref[...] = wide[...].astype(jnp.bfloat16)


def channel_kernel(
    me_ref, taps_ref, skip_ref, recv_ref, edge_ref, fwd_ref, inv_ref, cos_ref, sin_ref, out_ref, wide
):
    shards = out_ref.shape[0]
    lanes = out_ref.shape[1]
    me = me_ref[0]
    wide[...] = recv_ref[...].astype(jnp.float32)
    plane = lambda r: wide[pl.ds(r, shards, stride=ROWS), :]
    lane = lax.broadcasted_iota(jnp.int32, (shards, lanes), 1)
    shard = lax.broadcasted_iota(jnp.int32, (shards, lanes), 0)

    def delayed(x, steps):
        same = pltpu.roll(x, steps, 1)
        before = jnp.where(shard == 0, 0.0, pltpu.roll(same, 1, 0))
        return jnp.where(lane < steps, before, same)

    def short_conv(i):
        x = plane(i)
        tap = taps_ref[i, pl.ds(me, 1), :]
        return tap[:, 0:1] * x + tap[:, 1:2] * delayed(x, 1) + tap[:, 2:3] * delayed(x, 2)

    query, keyed, value = short_conv(0), short_conv(1), short_conv(2)
    mixed = (keyed * value).astype(jnp.bfloat16)
    dot = functools.partial(lax.dot_general, preferred_element_type=jnp.float32)
    edge = edge_ref[...]
    cos, sin = cos_ref[...], sin_ref[...]
    size = cos.shape[1]
    part = dot(mixed, edge, (((0,), (0,)), ((), ())))
    a_re, a_im = part[:, :size], part[:, size:]
    b = jnp.concatenate([a_re * cos - a_im * sin, a_re * sin + a_im * cos], axis=0)
    spec = dot(fwd_ref[...], b.astype(jnp.bfloat16), (((1,), (0,)), ((), ())))
    s_re, s_im = spec[:lanes], spec[lanes:]
    f_re = jnp.concatenate([plane(3), plane(4)], axis=1)
    f_im = jnp.concatenate([plane(5), plane(6)], axis=1)
    prod = jnp.concatenate([s_re * f_re - s_im * f_im, s_re * f_im + s_im * f_re], axis=0)
    back = dot(inv_ref[...], prod.astype(jnp.bfloat16), (((1,), (0,)), ((), ())))
    c_re, c_im = back[:lanes], back[lanes:]
    d = jnp.concatenate([c_re * cos + c_im * sin, c_im * cos - c_re * sin], axis=1)
    long_out = dot(edge, d.astype(jnp.bfloat16), (((1,), (1,)), ((), ())))
    long_out = long_out * (1.0 / (size * lanes))
    out_ref[...] = query * (long_out + skip_ref[me] * mixed.astype(jnp.float32))


def pack(proj, filter_spectrum):
    chans, lanes = proj.shape[1], proj.shape[2]
    return pl.pallas_call(
        pack_kernel,
        out_shape=jax.ShapeDtypeStruct((chans * ROWS, lanes), jnp.bfloat16),
        scratch_shapes=[pltpu.VMEM((chans * ROWS, lanes), jnp.float32)],
        compiler_params=pltpu.CompilerParams(vmem_limit_bytes=16 * 2**20),
    )(proj, filter_spectrum)


def convolve(me, taps, skip, recv, tabs):
    lanes = recv.shape[1]
    shards = recv.shape[0] // ROWS
    vmem = pl.BlockSpec(memory_space=pltpu.VMEM)
    smem = pl.BlockSpec(memory_space=pltpu.SMEM)
    return pl.pallas_call(
        channel_kernel,
        out_shape=jax.ShapeDtypeStruct((shards, lanes), jnp.float32),
        in_specs=[smem, vmem, smem, vmem] + [vmem] * len(tabs),
        out_specs=vmem,
        scratch_shapes=[pltpu.VMEM((shards * ROWS, lanes), jnp.float32)],
        compiler_params=pltpu.CompilerParams(vmem_limit_bytes=16 * 2**20),
    )(me, taps, skip, recv, *tabs)


def per_device(proj, short_filter, skip_gain, norm_gain, filter_spectrum):
    chans, tok = proj.shape[1], proj.shape[2]
    peers = lax.axis_size("seq")
    groups = lax.axis_size("tp")
    me = lax.axis_index("seq").astype(jnp.int32).reshape(1)
    tabs = tables(peers, tok)
    sent = pack(proj, filter_spectrum).reshape(peers, ROWS, tok)
    recv = lax.all_to_all(sent, "seq", split_axis=0, concat_axis=0, tiled=True)
    pre = convolve(me, short_filter, skip_gain, recv.reshape(peers * ROWS, tok), tabs)
    pre = lax.all_to_all(
        pre.reshape(peers, 1, tok), "seq", split_axis=0, concat_axis=0, tiled=True
    ).reshape(chans, tok)
    meansq = lax.psum(jnp.sum(pre * pre, axis=0), "tp") / (chans * groups)
    return (pre * lax.rsqrt(meansq + 1e-05)[None, :] * norm_gain[:, None]).astype(jnp.bfloat16)


def solution(mesh):
    return jax.shard_map(
        per_device,
        mesh=mesh,
        in_specs=(
            P(None, "tp", "seq"),
            P(None, "tp", None),
            P("tp"),
            P("tp"),
            P(None, "tp", "seq"),
        ),
        out_specs=P("tp", "seq"),
        check_vma=False,
    )
```

time: 224 us -> 66 us (0.29)
  waiting for transfers between devices: 96.9 us -> 14.1 us
  starting transfers between devices: 65.4 us -> 18.6 us
  blocking collectives: 43.4 us -> 26.5 us
  matrix products: 8.01 us -> 0 us
  local copies, waits for them, and re-layouts: 6.84 us -> 3.28 us
  Pallas kernels: 0 us -> 2.31 us
    all_to_all x8 -> x1, waiting for transfers between devices: 93.4 us -> 14.1 us  [per_device(): recv = lax.all_to_all(sent, 'seq', split_axis=0, concat_axis=0, tiled=True)]
    all_to_all x8 -> x1, starting transfers between devices: 60 us -> 18.6 us  [per_device(): recv = lax.all_to_all(sent, 'seq', split_axis=0, concat_axis=0, tiled=True)]
    all_to_all x2 -> x1, blocking collectives: 35 us -> 18 us  [per_device(): lax.all_to_all(pre.reshape(peers, 1, tok), 'seq', split_axis=0, concat_ax...]
    dot_general x12 -> x0, matrix products: 8.01 us -> none  [the longest x1 1.42 us: per_device(): first_im = jnp.einsum('csb,sk->ckb', columns, coarse_s, precision=HIGH)]
    ppermute x1 -> x0, starting transfers between devices: 5.39 us -> none  [shifted(): return lax.ppermute(block, axis, route)]
    ppermute x1 -> x0, waiting for transfers between devices: 3.5 us -> none  [shifted(): return lax.ppermute(block, axis, route)]
    pallas_call x0 -> x2, Pallas kernels: none -> 2.31 us  [the longest x1 1.46 us: convolve(): pl.pallas_call(channel_kernel, out_shape=jax.ShapeDtypeStruct((shards, la...]
  transfers between devices with their start and end apart: 9 -> 1, of which waited for: 9 -> 1; matrix products, arithmetic and copies ran while one was open for 2% -> 0% of each run, Pallas kernels for 0% -> 0%
where the time goes in v1:
time: 66 us; the launch traced here: 65.5 us
  blocking collectives  26.5 us (40%)
  starting transfers between devices  18.6 us (28%)
  waiting for transfers between devices  14.1 us (21%)
  local copies, waits for them, and re-layouts  3.28 us (5%)
  Pallas kernels  2.31 us (4%)
  other arithmetic  0.74 us (1%)
    all_to_all x1, starting transfers between devices, per_device(): recv = lax.all_to_all(sent, 'seq', split_axis=0, concat_axis=0, tiled=True)  18.6 us
    all_to_all x1, blocking collectives, per_device(): lax.all_to_all(pre.reshape(peers, 1, tok), 'seq', split_axis=0, concat_ax...  18 us
    all_to_all x1, waiting for transfers between devices, per_device(): recv = lax.all_to_all(sent, 'seq', split_axis=0, concat_axis=0, tiled=True)  14.1 us
    psum x1, blocking collectives, per_device(): meansq = lax.psum(jnp.sum(pre * pre, axis=0), 'tp') / (chans * groups)  8.47 us
    unnamed x21, local copies, waits for them, and re-layouts  3.28 us
    pallas_call x1, Pallas kernels, convolve(): pl.pallas_call(channel_kernel, out_shape=jax.ShapeDtypeStruct((shards, la...  1.46 us
  transfers between devices with their start and end apart: 1, of which 1 were waited for; matrix products, arithmetic and copies ran while one was open for 0% of the time, Pallas kernels for 0%

profile of v1, /device:TPU:1, one launch (start us, length us, event | category | flops | bytes accessed | tf_op | source)
XLA Modules:
  0.0 65.5 jit_solution(10162555148857213883)
XLA Ops:
  0.0 0.0 copy-start
  0.0 0.9 %copy-done = f32[2,128,256]{2,1,0:T(8,128)S(1)} copy-done((f32[2,128,256]{2,1,0:T(8,128)S(1)}, f32[2,128,256]{2,1,0:T(8,128)}, u32[]{:S(2)}) %copy-start) | copy-done | bytes 262168
  1.0 0.0 copy-start.6
  1.0 0.9 %copy-done.6 = bf16[3,128,128]{2,1,0:T(8,128)(2,1)S(1)} copy-done((bf16[3,128,128]{2,1,0:T(8,128)(2,1)S(1)}, bf16[3,128,128]{2,1,0:T(8,128)(2,1)}, u32[]{:S(2)}) %copy-start.6) | copy-done | bytes 98328
  1.8 0.0 copy-start.8
  1.8 0.8 %shard_map.100 = bf16[1024,128]{1,0:T(8,128)(2,1)} custom-call(bf16[3,128,128]{2,1,0:T(8,128)(2,1)S(1)} %copy-done.6, f32[2,128,256]{2,1,0:T(8,128)S(1)} %copy-done), custom_call_target="tpu_custom_call" | custom-call | tf_op jit(solution)/shard_map/pallas_call | solution.py:89
  2.7 0.0 copy-start.2
  2.7 0.0 copy-start.3
  2.7 18.6 %all-to-all-start = ((bf16[128,8,128]{2,1,0:T(8,128)(2,1)}), bf16[128,8,128]{2,1,0:T(8,128)(2,1)S(1)}, u32[]{:S(2)}, u32[]{:S(2)}) async-start(bf16[128,8,128]{2,1,0:T(8,128)(2,1)} %bitcast.1), calls=%async_computation | async-start | bytes 524288 | tf_op jit(solution)/shard_map/all_to_all | solution.py:119
  21.3 0.0 copy-start.1
  21.3 0.0 copy-done.8
  21.3 0.1 copy.12.taps_ref
  21.5 14.1 %all-to-all-done = bf16[128,8,128]{2,1,0:T(8,128)(2,1)S(1)} async-done(((bf16[128,8,128]{2,1,0:T(8,128)(2,1)}), bf16[128,8,128]{2,1,0:T(8,128)(2,1)S(1)}, u32[]{:S(2)}, u32[]{:S(2)}) %all-to-all-start) | async-done | bytes 262176 | tf_op jit(solution)/shard_map/all_to_all | solution.py:119
  35.5 0.0 copy-done.2
  35.5 0.0 copy-done.3
  35.5 0.0 copy-done.4
  35.5 0.0 copy-done.5
  35.5 0.0 copy-done.1
  35.5 0.6 copy-done.7
  36.2 1.5 %shard_map.101 = f32[128,128]{1,0:T(8,128)S(1)} custom-call(s32[1]{0:T(128)} %bitcast.me_ref, f32[3,128,3]{2,1,0:T(8,128)S(1)} %copy.12.taps_ref, f32[128]{0:T(128)S(1)} %copy-done.7, bf16[1024,128]{1,0:T(8,128)(2,1)S(1)} %bitcast.7, bf16[128,512]{1,0:T(8,128)(2,1)S(1)} %copy-done.1, bf16[256,256]{1,0:T(8,128)(2,1)S(1)} %copy-done.2, ...), custom_call_target="tpu_custom_call" | custom-call | tf_op jit(solution)/shard_map/pallas_call | solution.py:102
  37.6 18.0 %all_to_all.10 = f32[128,1,128]{2,1,0:T(1,128)S(1)} all-to-all(f32[128,1,128]{2,1,0:T(1,128)S(1)} %bitcast.8), channel_id=1, replica_groups=mesh['seq'=128,'tp'=4] {'seq'}, dimensions={0} | all-to-all | bytes 131072 | tf_op jit(solution)/shard_map/all_to_all | solution.py:121
  55.7 8.5 %psum.7 = f32[128]{0:T(128)S(1)} all-reduce(f32[128]{0:T(128)S(1)} %multiply_reduce_fusion), channel_id=1, replica_groups=mesh['seq'=128,'tp'=4] {'tp'}, use_global_device_ids=true, to_apply=%region_1.0 | all-reduce | flops 128 | bytes 1024 | tf_op jit(solution)/shard_map/psum | solution.py:124
  64.1 0.6 copy-done.9
  64.8 0.7 %multiply_convert_fusion = bf16[128,128]{1,0:T(8,128)(2,1)} fusion(f32[128,128]{1,0:T(8,128)S(1)} %bitcast.10, f32[128]{0:T(128)S(1)} %copy-done.9, f32[128]{0:T(128)S(1)} %add_rsqrt_fusion), kind=kLoop, calls=%fused_computation | loop fusion | flops 49152 | bytes 99328 | tf_op jit(solution)/shard_map/convert_element_type | solution.py:125
  (6 shorter events, 0.0 us)
Async XLA Ops:
  0.0 0.9 %copy-start = (f32[2,128,256]{2,1,0:T(8,128)S(1)}, f32[2,128,256]{2,1,0:T(8,128)}, u32[]{:S(2)}) copy-start(f32[2,128,256]{2,1,0:T(8,128)} %filt_ref.1) | copy-start | bytes 786436
  1.0 0.9 %copy-start.6 = (bf16[3,128,128]{2,1,0:T(8,128)(2,1)S(1)}, bf16[3,128,128]{2,1,0:T(8,128)(2,1)}, u32[]{:S(2)}) copy-start(bf16[3,128,128]{2,1,0:T(8,128)(2,1)} %proj_ref.1) | copy-start | bytes 294916
  1.8 19.5 %copy-start.8 = (f32[3,128,3]{1,2,0:T(4,128)S(1)}, f32[3,128,3]{1,2,0:T(4,128)}, u32[]{:S(2)}) copy-start(f32[3,128,3]{1,2,0:T(4,128)} %param.11) | copy-start | bytes 13828
  2.7 32.8 %copy-start.2 = (bf16[256,256]{1,0:T(8,128)(2,1)S(1)}, bf16[256,256]{1,0:T(8,128)(2,1)}, u32[]{:S(2)}) copy-start(bf16[256,256]{1,0:T(8,128)(2,1)} %constant.24.clone.fwd_ref) | copy-start | bytes 393220
  2.7 32.8 %copy-start.3 = (bf16[256,256]{1,0:T(8,128)(2,1)S(1)}, bf16[256,256]{1,0:T(8,128)(2,1)}, u32[]{:S(2)}) copy-start(bf16[256,256]{1,0:T(8,128)(2,1)} %constant.25.clone.inv_ref) | copy-start | bytes 393220
  2.7 32.8 %copy-start.4 = (f32[128,256]{1,0:T(8,128)S(1)}, f32[128,256]{1,0:T(8,128)}, u32[]{:S(2)}) copy-start(f32[128,256]{1,0:T(8,128)} %constant.26.clone.cos_ref) | copy-start | bytes 393220
  2.7 32.8 %copy-start.5 = (f32[128,256]{1,0:T(8,128)S(1)}, f32[128,256]{1,0:T(8,128)}, u32[]{:S(2)}) copy-start(f32[128,256]{1,0:T(8,128)} %constant.27.clone.sin_ref) | copy-start | bytes 393220
  2.7 32.8 %all-to-all-start = ((bf16[128,8,128]{2,1,0:T(8,128)(2,1)}), bf16[128,8,128]{2,1,0:T(8,128)(2,1)S(1)}, u32[]{:S(2)}, u32[]{:S(2)}) async-start(bf16[128,8,128]{2,1,0:T(8,128)(2,1)} %bitcast.1), calls=%async_computation | async-start | bytes 524288 | tf_op jit(solution)/shard_map/all_to_all | solution.py:119
  21.3 14.3 %copy-start.1 = (bf16[128,512]{1,0:T(8,128)(2,1)S(1)}, bf16[128,512]{1,0:T(8,128)(2,1)}, u32[]{:S(2)}) copy-start(bf16[128,512]{1,0:T(8,128)(2,1)} %constant.23.clone.edge_ref) | copy-start | bytes 393220
  35.5 0.7 %copy-start.7 = (f32[128]{0:T(128)S(1)}, f32[128]{0:T(128)}, u32[]{:S(2)}) copy-start(f32[128]{0:T(128)} %skip_ref.1) | copy-start | bytes 1540
  64.1 0.7 %copy-start.9 = (f32[128]{0:T(128)S(1)}, f32[128]{0:T(128)}, u32[]{:S(2)}) copy-start(f32[128]{0:T(128)} %param.13) | copy-start | bytes 1540

commit v2 on v1

v2 whole, which is shorter than its diff:
```python
import functools

import jax
import jax.numpy as jnp
import numpy as np
from jax import lax
from jax.experimental import pallas as pl
from jax.experimental.pallas import tpu as pltpu
from jax.sharding import PartitionSpec as P

ROWS = 8
CHUNKS = 4


def tables(n_coarse, n_fine):
    total = 2 * n_coarse * n_fine
    n1 = np.arange(n_coarse)
    k1 = np.arange(2 * n_coarse)
    n2 = np.arange(n_fine)
    first = 2.0 * np.pi * (np.outer(n1, k1) % (2 * n_coarse)) / (2 * n_coarse)
    edge = np.concatenate([np.cos(first), -np.sin(first)], axis=1)
    inner = 2.0 * np.pi * (np.outer(n2, n2) % n_fine) / n_fine
    w_re, w_im = np.cos(inner), -np.sin(inner)
    inner = np.concatenate([w_re, w_im], axis=1)
    half = n_fine // 2
    turn = 2.0 * np.pi * (np.outer(n2, k1) % total) / total
    turns = np.concatenate([np.cos(turn), -np.sin(turn)], axis=1)
    coarse = turns.astype(jnp.bfloat16).astype(np.float64)
    rows = [edge, np.concatenate([inner[:half], inner[half:]], axis=1), coarse, turns - coarse]
    return jnp.asarray(np.concatenate(rows, axis=0), jnp.bfloat16)


def pack_kernel(
    proj_hbm, filt_hbm, taps_hbm, skip_hbm, gain_hbm, out_hbm,
    proj_ref, filt_ref, taps_ref, skip_ref, gain_ref, wide, out_ref, sem_in, sem_out, sem_small
):
    chans = proj_ref.shape[1]
    lanes = proj_ref.shape[2]
    size = chans // CHUNKS
    small = [
        pltpu.make_async_copy(taps_hbm, taps_ref, sem_small.at[0]),
        pltpu.make_async_copy(skip_hbm, skip_ref, sem_small.at[1]),
        pltpu.make_async_copy(gain_hbm, gain_ref, sem_small.at[2]),
    ]
    for copy in small:
        copy.start()
    loads = []
    for chunk in range(CHUNKS):
        part = pl.ds(chunk * size, size)
        loads.append([
            pltpu.make_async_copy(proj_hbm.at[:, part], proj_ref.at[:, part], sem_in.at[0, chunk]),
            pltpu.make_async_copy(filt_hbm.at[:, part], filt_ref.at[:, part], sem_in.at[1, chunk]),
        ])
        for copy in loads[-1]:
            copy.start()
    for copy in small:
        copy.wait()
    me = lax.axis_index("seq")
    lane = lax.broadcasted_iota(jnp.int32, (1, lanes), 1)
    own_row = jnp.zeros((1, lanes), jnp.float32)
    planes = [taps_ref[i, m : m + 1, :] for i in range(3) for m in range(3)]
    for p, values in enumerate(planes + [skip_ref[...], gain_ref[...]]):
        own = jnp.sum(jnp.where(lane == me, values, 0.0), axis=1, keepdims=True)
        for k in range(3):
            piece = own.astype(jnp.bfloat16).astype(jnp.float32)
            own_row = jnp.where(lane == 16 * k + p, piece, own_row)
            own = own - piece
    stores = []
    for chunk in range(CHUNKS):
        for copy in loads[chunk]:
            copy.wait()
        base = chunk * size
        rows = pl.ds(base * ROWS, size * ROWS)
        row = lambda r: pl.ds(base * ROWS + r, size, stride=ROWS)
        for i in range(3):
            wide[row(i), :] = proj_ref[i, base : base + size].astype(jnp.float32)
        for part in range(2):
            for half in range(2):
                wide[row(3 + 2 * part + half), :] = filt_ref[
                    part, base : base + size, lanes * half : lanes * (half + 1)
                ]
        wide[row(7), :] = jnp.broadcast_to(own_row, (size, lanes))
        out_ref[rows, :] = wide[rows, :].astype(jnp.bfloat16)
        stores.append(pltpu.make_async_copy(out_ref.at[rows], out_hbm.at[rows], sem_out.at[chunk]))
        stores[-1].start()
    for copy in stores:
        copy.wait()


def channel_kernel(
    recv_ref, waves_ref, out_ref, gain_ref, wide
):
    shards = out_ref.shape[0]
    lanes = out_ref.shape[1]
    wide[...] = recv_ref[...].astype(jnp.float32)
    plane = lambda r: wide[pl.ds(r, shards, stride=ROWS), :]
    me = lax.axis_index("seq")
    merge = lambda x: x + pltpu.roll(x, lanes - 16, 1) + pltpu.roll(x, lanes - 32, 1)
    gain_ref[...] = jnp.broadcast_to(merge(plane(7))[:, 10:11], (shards, lanes))
    own = merge(wide[pl.ds(me * ROWS, ROWS), :][7:8, :])
    param = lambda p: jnp.broadcast_to(own[:, p : p + 1], (1, lanes))
    lane = lax.broadcasted_iota(jnp.int32, (shards, lanes), 1)
    shard = lax.broadcasted_iota(jnp.int32, (shards, lanes), 0)

    def delayed(x, steps):
        same = pltpu.roll(x, steps, 1)
        before = jnp.where(shard == 0, 0.0, pltpu.roll(same, 1, 0))
        return jnp.where(lane < steps, before, same)

    def short_conv(i):
        x = plane(i)
        tap = lambda m: param(3 * i + m)
        return tap(0) * x + tap(1) * delayed(x, 1) + tap(2) * delayed(x, 2)

    query, keyed, value = short_conv(0), short_conv(1), short_conv(2)
    mixed = (keyed * value).astype(jnp.bfloat16)
    dot = functools.partial(lax.dot_general, preferred_element_type=jnp.float32)
    size = 2 * shards
    edge = waves_ref[:shards, :]
    at = shards + lanes // 2
    inner = waves_ref[shards:at, :]
    inner = jnp.concatenate([inner[:, : 2 * lanes], inner[:, 2 * lanes :]], axis=0)
    w_re, w_im = inner[:, :lanes], inner[:, lanes:]
    square = lambda a, b, c, d: jnp.concatenate(
        [jnp.concatenate([a, b], axis=1), jnp.concatenate([c, d], axis=1)], axis=0
    )
    fwd, inv = square(w_re, -w_im, w_im, w_re), square(w_re, w_im, -w_im, w_re)
    turns = waves_ref[at : at + lanes, :].astype(jnp.float32)
    turns = turns + waves_ref[at + lanes :, :].astype(jnp.float32)
    cos, sin = turns[:, :size], turns[:, size:]
    part = dot(mixed, edge, (((0,), (0,)), ((), ())))
    a_re, a_im = part[:, :size], part[:, size:]
    b = jnp.concatenate([a_re * cos - a_im * sin, a_re * sin + a_im * cos], axis=0)
    spec = dot(fwd, b.astype(jnp.bfloat16), (((1,), (0,)), ((), ())))
    s_re, s_im = spec[:lanes], spec[lanes:]
    f_re = jnp.concatenate([plane(3), plane(4)], axis=1)
    f_im = jnp.concatenate([plane(5), plane(6)], axis=1)
    prod = jnp.concatenate([s_re * f_re - s_im * f_im, s_re * f_im + s_im * f_re], axis=0)
    back = dot(inv, prod.astype(jnp.bfloat16), (((1,), (0,)), ((), ())))
    c_re, c_im = back[:lanes], back[lanes:]
    d = jnp.concatenate([c_re * cos + c_im * sin, c_im * cos - c_re * sin], axis=1)
    long_out = dot(edge, d.astype(jnp.bfloat16), (((1,), (1,)), ((), ())))
    long_out = long_out * (1.0 / (size * lanes))
    out_ref[...] = query * (long_out + param(9) * mixed.astype(jnp.float32))


def pack(proj, filter_spectrum, taps, skip, gain):
    chans, lanes = proj.shape[1], proj.shape[2]
    hbm = pl.BlockSpec(memory_space=pltpu.HBM)
    inputs = (proj, filter_spectrum, taps, skip, gain)
    return pl.pallas_call(
        pack_kernel,
        out_shape=jax.ShapeDtypeStruct((chans * ROWS, lanes), jnp.bfloat16),
        in_specs=[hbm] * len(inputs),
        out_specs=hbm,
        scratch_shapes=[pltpu.VMEM(x.shape, x.dtype) for x in inputs]
        + [
            pltpu.VMEM((chans * ROWS, lanes), jnp.float32),
            pltpu.VMEM((chans * ROWS, lanes), jnp.bfloat16),
            pltpu.SemaphoreType.DMA((2, CHUNKS)),
            pltpu.SemaphoreType.DMA((CHUNKS,)),
            pltpu.SemaphoreType.DMA((3,)),
        ],
        compiler_params=pltpu.CompilerParams(vmem_limit_bytes=64 * 2**20),
    )(*inputs)


def convolve(recv, waves):
    lanes = recv.shape[1]
    shards = recv.shape[0] // ROWS
    vmem = pl.BlockSpec(memory_space=pltpu.VMEM)
    return pl.pallas_call(
        channel_kernel,
        out_shape=(jax.ShapeDtypeStruct((shards, lanes), jnp.float32),) * 2,
        in_specs=[vmem] * 2,
        out_specs=(vmem,) * 2,
        scratch_shapes=[pltpu.VMEM((shards * ROWS, lanes), jnp.float32)],
        compiler_params=pltpu.CompilerParams(vmem_limit_bytes=16 * 2**20),
    )(recv, waves)


def per_device(proj, short_filter, skip_gain, norm_gain, filter_spectrum):
    chans, tok = proj.shape[1], proj.shape[2]
    peers = lax.axis_size("seq")
    groups = lax.axis_size("tp")
    waves = tables(peers, tok)
    taps = jnp.swapaxes(short_filter, 1, 2)
    sent = pack(proj, filter_spectrum, taps, skip_gain[None], norm_gain[None])
    recv = lax.all_to_all(
        sent.reshape(peers, ROWS, tok), "seq", split_axis=0, concat_axis=0, tiled=True
    )
    pre, gain = convolve(recv.reshape(peers * ROWS, tok), waves)
    pre = lax.all_to_all(
        pre.reshape(peers, 1, tok), "seq", split_axis=0, concat_axis=0, tiled=True
    ).reshape(chans, tok)
    meansq = lax.psum(jnp.sum(pre * pre, axis=0), "tp") / (chans * groups)
    return (pre * lax.rsqrt(meansq + 1e-05)[None, :] * gain).astype(jnp.bfloat16)


def solution(mesh):
    return jax.shard_map(
        per_device,
        mesh=mesh,
        in_specs=(
            P(None, "tp", "seq"),
            P(None, "tp", None),
            P("tp"),
            P("tp"),
            P(None, "tp", "seq"),
        ),
        out_specs=P("tp", "seq"),
        check_vma=False,
    )
```

time: 66 us -> 63.4 us (0.961)
  blocking collectives: 26.5 us -> 59.2 us
  starting transfers between devices: 18.6 us -> 0 us
  waiting for transfers between devices: 14.1 us -> 0 us
  local copies, waits for them, and re-layouts: 3.28 us -> 0.01 us
    all_to_all x0 -> x1, blocking collectives: none -> 32.8 us  [per_device(): lax.all_to_all(sent.reshape(peers, ROWS, tok), 'seq', split_axis=0, conca...]
    all_to_all x1 -> x0, starting transfers between devices: 18.6 us -> none  [per_device(): recv = lax.all_to_all(sent, 'seq', split_axis=0, concat_axis=0, tiled=True)]
    all_to_all x1 -> x0, waiting for transfers between devices: 14.1 us -> none  [per_device(): recv = lax.all_to_all(sent, 'seq', split_axis=0, concat_axis=0, tiled=True)]
    unnamed x21 -> x2, local copies, waits for them, and re-layouts: 3.28 us -> 0.01 us
    pallas_call x1, Pallas kernels: 0.85 us -> 1.84 us  [pack(): pl.pallas_call(pack_kernel, out_shape=jax.ShapeDtypeStruct((chans * ROWS,...]
  transfers between devices with their start and end apart: 1 -> 0, of which waited for: 1 -> 0; matrix products, arithmetic and copies ran while one was open for 0% -> 0% of each run, Pallas kernels for 0% -> 0%
where the time goes in v2:
time: 63.4 us; the launch traced here: 62.8 us
  blocking collectives  59.2 us (93%)
  Pallas kernels  2.89 us (5%)
  other arithmetic  0.68 us (1%)
    all_to_all x1, blocking collectives, per_device(): lax.all_to_all(sent.reshape(peers, ROWS, tok), 'seq', split_axis=0, conca...  32.8 us
    all_to_all x1, blocking collectives, per_device(): lax.all_to_all(pre.reshape(peers, 1, tok), 'seq', split_axis=0, concat_ax...  18 us
    psum x1, blocking collectives, per_device(): meansq = lax.psum(jnp.sum(pre * pre, axis=0), 'tp') / (chans * groups)  8.47 us
    pallas_call x1, Pallas kernels, pack(): pl.pallas_call(pack_kernel, out_shape=jax.ShapeDtypeStruct((chans * ROWS,...  1.84 us

profile of v2, /device:TPU:1, one launch (start us, length us, event | category | flops | bytes accessed | tf_op | source)
XLA Modules:
  0.0 62.8 jit_solution(2616959248976830761)
XLA Ops:
  0.0 1.8 %shard_map.64 = bf16[1024,128]{1,0:T(8,128)(2,1)} custom-call(bf16[3,128,128]{2,1,0:T(8,128)(2,1)} %proj_hbm.1, f32[2,128,256]{2,1,0:T(8,128)} %filt_hbm.1, f32[3,3,128]{2,1,0:T(4,128)} %bitcast.14, f32[1,128]{1,0:T(1,128)} %bitcast.15, f32[1,128]{1,0:T(1,128)} %bitcast.16), custom_call_target="tpu_custom_call" | custom-call | tf_op jit(solution)/shard_map/pallas_call | solution.py:151
  1.8 0.0 copy-start
  1.9 32.8 %all_to_all.10 = bf16[128,8,128]{2,1,0:T(8,128)(2,1)S(1)} all-to-all(bf16[128,8,128]{2,1,0:T(8,128)(2,1)} %bitcast.11), channel_id=1, replica_groups=mesh['seq'=128,'tp'=4] {'seq'}, dimensions={0} | all-to-all | bytes 524288 | tf_op jit(solution)/shard_map/all_to_all | solution.py:189
  34.6 0.0 copy-done
  34.6 1.1 %shard_map.65 = (f32[128,128]{1,0:T(8,128)S(1)}, f32[128,128]{1,0:T(8,128)S(1)}) custom-call(bf16[1024,128]{1,0:T(8,128)(2,1)S(1)} %bitcast.9, bf16[448,512]{1,0:T(8,128)(2,1)S(1)} %copy-done), custom_call_target="tpu_custom_call" | custom-call | tf_op jit(solution)/shard_map/pallas_call | solution.py:172
  35.7 18.0 %all_to_all.11 = f32[128,1,128]{2,1,0:T(1,128)S(1)} all-to-all(f32[128,1,128]{2,1,0:T(1,128)S(1)} %bitcast.10), channel_id=1, replica_groups=mesh['seq'=128,'tp'=4] {'seq'}, dimensions={0} | all-to-all | bytes 131072 | tf_op jit(solution)/shard_map/all_to_all | solution.py:193
  53.7 8.5 %psum.7 = f32[128]{0:T(128)S(1)} all-reduce(f32[128]{0:T(128)S(1)} %multiply_reduce_fusion), channel_id=1, replica_groups=mesh['seq'=128,'tp'=4] {'tp'}, use_global_device_ids=true, to_apply=%region_1.0 | all-reduce | flops 128 | bytes 1024 | tf_op jit(solution)/shard_map/psum | solution.py:196
  62.2 0.6 %multiply_convert_fusion = bf16[128,128]{1,0:T(8,128)(2,1)} fusion(f32[128,128]{1,0:T(8,128)S(1)} %get-tuple-element.8, f32[128,128]{1,0:T(8,128)S(1)} %bitcast.13, f32[128]{0:T(128)S(1)} %add_rsqrt_fusion), kind=kLoop, calls=%fused_computation | loop fusion | flops 49152 | bytes 164352 | tf_op jit(solution)/shard_map/convert_element_type | solution.py:197
  (2 shorter events, 0.0 us)
Async XLA Ops:
  1.8 32.8 %copy-start = (bf16[448,512]{1,0:T(8,128)(2,1)S(1)}, bf16[448,512]{1,0:T(8,128)(2,1)}, u32[]{:S(2)}) copy-start(bf16[448,512]{1,0:T(8,128)(2,1)} %constant.9.clone.waves_ref) | copy-start | bytes 1376260

commit v3 on v2

--- a/solution.py
+++ b/solution.py
@@ -17,22 +17,20 @@
     n1 = np.arange(n_coarse)
     k1 = np.arange(2 * n_coarse)
     n2 = np.arange(n_fine)
-    first = 2.0 * np.pi * (np.outer(n1, k1) % (2 * n_coarse)) / (2 * n_coarse)
+    turn = 2.0 * np.pi * (np.outer(n2, k1) % total) / total
+    first = 2.0 * np.pi * (np.outer(n1, k1[:n_coarse]) % (2 * n_coarse)) / (2 * n_coarse)
     edge = np.concatenate([np.cos(first), -np.sin(first)], axis=1)
     inner = 2.0 * np.pi * (np.outer(n2, n2) % n_fine) / n_fine
-    w_re, w_im = np.cos(inner), -np.sin(inner)
-    inner = np.concatenate([w_re, w_im], axis=1)
-    half = n_fine // 2
-    turn = 2.0 * np.pi * (np.outer(n2, k1) % total) / total
+    inner = np.concatenate([np.cos(inner), -np.sin(inner)], axis=1)
+    fold = lambda x: np.concatenate([x[: len(x) // 2], x[len(x) // 2 :]], axis=1)
     turns = np.concatenate([np.cos(turn), -np.sin(turn)], axis=1)
-    coarse = turns.astype(jnp.bfloat16).astype(np.float64)
-    rows = [edge, np.concatenate([inner[:half], inner[half:]], axis=1), coarse, turns - coarse]
+    rows = [fold(edge), fold(inner), turns]
     return jnp.asarray(np.concatenate(rows, axis=0), jnp.bfloat16)
 
 
 def pack_kernel(
-    proj_hbm, filt_hbm, taps_hbm, skip_hbm, gain_hbm, out_hbm,
-    proj_ref, filt_ref, taps_ref, skip_ref, gain_ref, wide, out_ref, sem_in, sem_out, sem_small
+    proj_hbm, filt_hbm, taps_hbm, skip_hbm, gain_hbm, out_ref,
+    proj_ref, filt_ref, taps_ref, skip_ref, gain_ref, wide, sem_in, sem_small
 ):
     chans = proj_ref.shape[1]
     lanes = proj_ref.shape[2]
@@ -65,7 +63,6 @@
             piece = own.astype(jnp.bfloat16).astype(jnp.float32)
             own_row = jnp.where(lane == 16 * k + p, piece, own_row)
             own = own - piece
-    stores = []
     for chunk in range(CHUNKS):
         for copy in loads[chunk]:
             copy.wait()
@@ -81,10 +78,6 @@
                 ]
         wide[row(7), :] = jnp.broadcast_to(own_row, (size, lanes))
         out_ref[rows, :] = wide[rows, :].astype(jnp.bfloat16)
-        stores.append(pltpu.make_async_copy(out_ref.at[rows], out_hbm.at[rows], sem_out.at[chunk]))
-        stores[-1].start()
-    for copy in stores:
-        copy.wait()
 
 
 def channel_kernel(
@@ -116,17 +109,19 @@
     mixed = (keyed * value).astype(jnp.bfloat16)
     dot = functools.partial(lax.dot_general, preferred_element_type=jnp.float32)
     size = 2 * shards
-    edge = waves_ref[:shards, :]
-    at = shards + lanes // 2
-    inner = waves_ref[shards:at, :]
-    inner = jnp.concatenate([inner[:, : 2 * lanes], inner[:, 2 * lanes :]], axis=0)
+    unfold = lambda x: jnp.concatenate([x[:, :size], x[:, size:]], axis=0)
+    half = shards // 2
+    edge = unfold(waves_ref[:half, :])
+    flip = jnp.where(shard % 2 == 0, 1.0, -1.0).astype(jnp.bfloat16)
+    c, d = edge[:, :shards], edge[:, shards:]
+    edge = jnp.concatenate([c, c * flip, d, d * flip], axis=1)
+    inner = unfold(waves_ref[half : half + lanes // 2, :])
     w_re, w_im = inner[:, :lanes], inner[:, lanes:]
     square = lambda a, b, c, d: jnp.concatenate(
         [jnp.concatenate([a, b], axis=1), jnp.concatenate([c, d], axis=1)], axis=0
     )
     fwd, inv = square(w_re, -w_im, w_im, w_re), square(w_re, w_im, -w_im, w_re)
-    turns = waves_ref[at : at + lanes, :].astype(jnp.float32)
-    turns = turns + waves_ref[at + lanes :, :].astype(jnp.float32)
+    turns = waves_ref[half + lanes // 2 :, :].astype(jnp.float32)
     cos, sin = turns[:, :size], turns[:, size:]
     part = dot(mixed, edge, (((0,), (0,)), ((), ())))
     a_re, a_im = part[:, :size], part[:, size:]
@@ -152,17 +147,15 @@
         pack_kernel,
         out_shape=jax.ShapeDtypeStruct((chans * ROWS, lanes), jnp.bfloat16),
         in_specs=[hbm] * len(inputs),
-        out_specs=hbm,
+        out_specs=pl.BlockSpec(memory_space=pltpu.VMEM),
         scratch_shapes=[pltpu.VMEM(x.shape, x.dtype) for x in inputs]
         + [
             pltpu.VMEM((chans * ROWS, lanes), jnp.float32),
-            pltpu.VMEM((chans * ROWS, lanes), jnp.bfloat16),
             pltpu.SemaphoreType.DMA((2, CHUNKS)),
-            pltpu.SemaphoreType.DMA((CHUNKS,)),
             pltpu.SemaphoreType.DMA((3,)),
         ],
-        compiler_params=pltpu.CompilerParams(vmem_limit_bytes=64 * 2**20),
-    )(*inputs)
+        compiler_params=pltpu.CompilerParams(vmem_limit_bytes=16 * 2**20),
+    )(*(pltpu.with_memory_space_constraint(x, pltpu.HBM) for x in inputs))
 
 
 def convolve(recv, waves):
@@ -193,7 +186,9 @@
     pre = lax.all_to_all(
         pre.reshape(peers, 1, tok), "seq", split_axis=0, concat_axis=0, tiled=True
     ).reshape(chans, tok)
-    meansq = lax.psum(jnp.sum(pre * pre, axis=0), "tp") / (chans * groups)
+    squares = jnp.broadcast_to(jnp.sum(pre * pre, axis=0)[None, None], (groups, 1, tok))
+    squares = lax.all_to_all(squares, "tp", split_axis=0, concat_axis=0, tiled=True)
+    meansq = jnp.sum(squares[:, 0], axis=0) / (chans * groups)
     return (pre * lax.rsqrt(meansq + 1e-05)[None, :] * gain).astype(jnp.bfloat16)
 
 

time: 63.4 us -> 61.7 us (0.973)
  blocking collectives: 59.2 us -> 58.5 us
  Pallas kernels: 2.89 us -> 2.23 us
    psum x1 -> x0, blocking collectives: 8.47 us -> none  [per_device(): meansq = lax.psum(jnp.sum(pre * pre, axis=0), 'tp') / (chans * groups)]
    all_to_all x0 -> x1, blocking collectives: none -> 7.92 us  [per_device(): lax.all_to_all(squares, 'tp', split_axis=0, concat_axis=0, tiled=True)]
    pallas_call x1, Pallas kernels: 1.84 us -> 1.18 us  [pack(): pl.pallas_call(pack_kernel, out_shape=jax.ShapeDtypeStruct((chans * ROWS,...]
where the time goes in v3:
time: 61.7 us; the launch traced here: 61.4 us
  blocking collectives  58.5 us (95%)
  Pallas kernels  2.23 us (4%)
  other arithmetic  0.69 us (1%)
    all_to_all x1, blocking collectives, per_device(): lax.all_to_all(sent.reshape(peers, ROWS, tok), 'seq', split_axis=0, conca...  32.6 us
    all_to_all x1, blocking collectives, per_device(): lax.all_to_all(pre.reshape(peers, 1, tok), 'seq', split_axis=0, concat_ax...  17.9 us
    all_to_all x1, blocking collectives, per_device(): lax.all_to_all(squares, 'tp', split_axis=0, concat_axis=0, tiled=True)  7.92 us

profile of v3, /device:TPU:1, one launch (start us, length us, event | category | flops | bytes accessed | tf_op | source)
XLA Modules:
  0.0 61.4 jit_solution(3580325669615522745)
XLA Ops:
  0.0 1.2 %shard_map.64 = bf16[1024,128]{1,0:T(8,128)(2,1)S(1)} custom-call(bf16[3,128,128]{2,1,0:T(8,128)(2,1)} %proj_hbm.1, f32[2,128,256]{2,1,0:T(8,128)} %filt_hbm.1, f32[3,3,128]{2,1,0:T(4,128)} %bitcast.16, f32[1,128]{1,0:T(1,128)} %bitcast.17, f32[1,128]{1,0:T(1,128)} %bitcast.18), custom_call_target="tpu_custom_call" | custom-call | tf_op jit(solution)/shard_map/pallas_call | solution.py:146
  1.2 0.0 copy-start
  1.2 32.6 %all_to_all.15 = bf16[128,8,128]{2,1,0:T(8,128)(2,1)S(1)} all-to-all(bf16[128,8,128]{2,1,0:T(8,128)(2,1)S(1)} %bitcast.10), channel_id=1, replica_groups=mesh['seq'=128,'tp'=4] {'seq'}, dimensions={0} | all-to-all | bytes 524288 | tf_op jit(solution)/shard_map/all_to_all | solution.py:182
  33.8 0.0 copy-done
  33.9 1.0 %shard_map.65 = (f32[128,128]{1,0:T(8,128)S(1)}, f32[128,128]{1,0:T(8,128)S(1)}) custom-call(bf16[1024,128]{1,0:T(8,128)(2,1)S(1)} %bitcast.11, bf16[256,512]{1,0:T(8,128)(2,1)S(1)} %copy-done), custom_call_target="tpu_custom_call" | custom-call | tf_op jit(solution)/shard_map/pallas_call | solution.py:165
  34.9 17.9 %all_to_all.16 = f32[128,1,128]{2,1,0:T(1,128)S(1)} all-to-all(f32[128,1,128]{2,1,0:T(1,128)S(1)} %bitcast.12), channel_id=1, replica_groups=mesh['seq'=128,'tp'=4] {'seq'}, dimensions={0} | all-to-all | bytes 131072 | tf_op jit(solution)/shard_map/all_to_all | solution.py:186
  52.9 7.9 %all_to_all.17 = f32[4,1,128]{2,1,0:T(1,128)S(1)} all-to-all(f32[4,1,128]{2,1,0:T(1,128)S(1)} %broadcast_in_dim.15), channel_id=1, replica_groups=mesh['seq'=128,'tp'=4] {'tp'}, dimensions={0} | all-to-all | bytes 4096 | tf_op jit(solution)/shard_map/all_to_all | solution.py:190
  60.8 0.6 %multiply_convert_fusion = bf16[128,128]{1,0:T(8,128)(2,1)} fusion(f32[128,128]{1,0:T(8,128)S(1)} %get-tuple-element.8, f32[128,128]{1,0:T(8,128)S(1)} %bitcast.14, f32[128]{0:T(128)S(1)} %add_rsqrt_fusion), kind=kLoop, calls=%fused_computation | loop fusion | flops 49152 | bytes 164352 | tf_op jit(solution)/shard_map/convert_element_type | solution.py:192
  (4 shorter events, 0.1 us)
Async XLA Ops:
  1.2 32.7 %copy-start = (bf16[256,512]{1,0:T(8,128)(2,1)S(1)}, bf16[256,512]{1,0:T(8,128)(2,1)}, u32[]{:S(2)}) copy-start(bf16[256,512]{1,0:T(8,128)(2,1)} %constant.9.clone.waves_ref) | copy-start | bytes 786436

commit v4 on v3

v4 whole, which is shorter than its diff:
```python
import jax
import jax.numpy as jnp
import numpy as np
from jax import lax
from jax.experimental import pallas as pl
from jax.experimental.pallas import tpu as pltpu
from jax.sharding import PartitionSpec as P

ROWS = 6
EDGE_ROW = 5
CHUNKS = 2
PARAMS = 32


def tables(n_coarse, n_fine):
    total = 2 * n_coarse * n_fine
    n1 = np.arange(n_coarse)
    k1 = np.arange(2 * n_coarse)
    n2 = np.arange(n_fine)
    turn = 2.0 * np.pi * (np.outer(n2, k1) % total) / total
    first = 2.0 * np.pi * (np.outer(n1, k1[:n_coarse]) % (2 * n_coarse)) / (2 * n_coarse)
    edge = np.concatenate([np.cos(first), -np.sin(first)], axis=1)
    inner = 2.0 * np.pi * (np.outer(n2, n2) % n_fine) / n_fine
    inner = np.concatenate([np.cos(inner), -np.sin(inner)], axis=1)
    fold = lambda x: np.concatenate([x[: len(x) // 2], x[len(x) // 2 :]], axis=1)
    turns = np.concatenate([np.cos(turn), -np.sin(turn)], axis=1)
    rows = [fold(edge), fold(inner), turns]
    return jnp.asarray(np.concatenate(rows, axis=0), jnp.bfloat16)


def pack_kernel(
    proj_hbm, filt_hbm, taps_hbm, skip_hbm, gain_hbm, out_ref, factor_ref,
    proj_ref, filt_ref, small_ref, wide, sem_in, sem_small
):
    chans = proj_ref.shape[1]
    lanes = proj_ref.shape[2]
    size = chans // CHUNKS
    small = [
        pltpu.make_async_copy(taps_hbm.at[i], small_ref.at[pl.ds(3 * i, 3)], sem_small.at[i])
        for i in range(3)
    ] + [
        pltpu.make_async_copy(skip_hbm, small_ref.at[pl.ds(9, 1)], sem_small.at[3]),
        pltpu.make_async_copy(gain_hbm, small_ref.at[pl.ds(10, 1)], sem_small.at[4]),
    ]
    for copy in small:
        copy.start()
    loads = []
    for chunk in range(CHUNKS):
        part = pl.ds(chunk * size, size)
        loads.append([
            pltpu.make_async_copy(proj_hbm.at[:, part], proj_ref.at[:, part], sem_in.at[0, chunk]),
            pltpu.make_async_copy(filt_hbm.at[:, part], filt_ref.at[:, part], sem_in.at[1, chunk]),
        ])
        for copy in loads[-1]:
            copy.start()
    for copy in small:
        copy.wait()
    me = lax.axis_index("seq")
    lane = lax.broadcasted_iota(jnp.int32, (16, lanes), 1)
    param = lax.broadcasted_iota(jnp.int32, (16, lanes), 0)
    params = jnp.where(param < 11, small_ref[...], 0.0)
    columns = params.T
    own = jnp.sum(jnp.where(lane == me, params, 0.0), axis=1, keepdims=True)
    spread = jnp.zeros((16, lanes), jnp.float32)
    for k in range(3):
        piece = own.astype(jnp.bfloat16).astype(jnp.float32)
        spread = jnp.where(lane == PARAMS + 16 * k + param, piece, spread)
        own = own - piece
    own_row = jnp.sum(spread, axis=0, keepdims=True)
    lane = lax.broadcasted_iota(jnp.int32, (size, lanes), 1)
    for chunk in range(CHUNKS):
        for copy in loads[chunk]:
            copy.wait()
        base = chunk * size
        rows = pl.ds(base * ROWS, size * ROWS)
        row = lambda r: pl.ds(base * ROWS + r, size, stride=ROWS)
        raw = [proj_ref[i, base : base + size].astype(jnp.float32) for i in range(3)]

        once = [pltpu.roll(x, 1, 1) for x in raw]
        twice = [pltpu.roll(x, 2, 1) for x in raw]

        def conv(i):
            tap = lambda m: columns[base : base + size, 3 * i + m : 3 * i + m + 1]
            late = tap(1) * jnp.where(lane < 1, 0.0, once[i])
            return tap(0) * raw[i] + late + tap(2) * jnp.where(lane < 2, 0.0, twice[i])

        factor_ref[base : base + size, :] = jnp.where(lane < 2, 1.0, conv(0))
        wide[row(0), :] = conv(1) * conv(2)
        for part in range(2):
            for half in range(2):
                wide[row(1 + 2 * part + half), :] = filt_ref[
                    part, base : base + size, lanes * half : lanes * (half + 1)
                ]
        fourth = pltpu.roll(raw[0], 4, 1)
        heads = jnp.where(lane < 2, raw[1], jnp.where(lane < 4, twice[2], fourth))
        tails = jnp.where(lane < 2, twice[2], jnp.where(lane < 4, fourth, raw[1]))
        edges = jnp.where(lane < 14, pltpu.roll(tails, 10, 1), own_row)
        edges = jnp.where(lane < 8, heads, edges)
        wide[row(EDGE_ROW), :] = edges
        out_ref[rows, :] = wide[rows, :].astype(jnp.bfloat16)


def channel_kernel(recv_ref, waves_ref, out_ref, gain_ref, wide):
    shards = out_ref.shape[0]
    lanes = out_ref.shape[1]
    size = 2 * shards
    wide[...] = recv_ref[...].astype(jnp.float32)
    plane = lambda r: wide[pl.ds(r, shards, stride=ROWS), :]
    lane = lax.broadcasted_iota(jnp.int32, (shards, lanes), 1)
    shard = lax.broadcasted_iota(jnp.int32, (shards, lanes), 0)
    back = lambda x, steps: pltpu.roll(x, lanes - steps, 1)
    merge = lambda x: x + back(x, 16) + back(x, 32)

    edges = plane(EDGE_ROW)
    gain_ref[...] = jnp.broadcast_to(merge(edges)[:, PARAMS + 10 : PARAMS + 11], (shards, lanes))
    me = lax.axis_index("seq")
    own = merge(wide[pl.ds(me * ROWS + EDGE_ROW, 1), :])
    param = lambda p: jnp.broadcast_to(own[:, PARAMS + p : PARAMS + p + 1], (1, lanes))
    first = lax.broadcasted_iota(jnp.int32, (1, lanes), 1)
    tap = lambda m: jnp.where(
        first < 2, param(3 + m), jnp.where(first < 4, param(6 + m), param(m))
    )
    two_ago = back(jnp.where(shard == 0, 0.0, pltpu.roll(edges, 1, 0)), 8)
    one_ago = jnp.where(lane % 2 == 1, pltpu.roll(edges, 1, 1), back(two_ago, 1))
    conv = tap(0) * edges + tap(1) * one_ago + tap(2) * two_ago
    mixed = jnp.where(lane < 2, conv * back(conv, 2), plane(0)).astype(jnp.bfloat16)

    unfold = lambda x: jnp.concatenate([x[:, :size], x[:, size:]], axis=0)
    square = lambda a, b, c, d: jnp.concatenate(
        [jnp.concatenate([a, b], axis=1), jnp.concatenate([c, d], axis=1)], axis=0
    )
    dot = lambda a, b, dims: lax.dot_general(
        a, b, (dims, ((), ())), preferred_element_type=jnp.float32
    )
    half = shards // 2
    edge = unfold(waves_ref[:half, :])
    flip = jnp.where(shard % 2 == 0, 1.0, -1.0).astype(jnp.bfloat16)
    c, d = edge[:, :shards], edge[:, shards:]
    edge = jnp.concatenate([c, c * flip, d, d * flip], axis=1)
    inner = unfold(waves_ref[half : half + lanes // 2, :])
    w_re, w_im = inner[:, :lanes], inner[:, lanes:]
    fwd, inv = square(w_re, -w_im, w_im, w_re), square(w_re, w_im, -w_im, w_re)
    turns = waves_ref[half + lanes // 2 :, :].astype(jnp.float32)
    cos, sin = turns[:, :size], turns[:, size:]

    part = dot(mixed, edge, ((0,), (0,)))
    a_re, a_im = part[:, :size], part[:, size:]
    b = jnp.concatenate([a_re * cos - a_im * sin, a_re * sin + a_im * cos], axis=0)
    spec = dot(fwd, b.astype(jnp.bfloat16), ((1,), (0,)))
    s_re, s_im = spec[:lanes], spec[lanes:]
    f_re = jnp.concatenate([plane(1), plane(2)], axis=1)
    f_im = jnp.concatenate([plane(3), plane(4)], axis=1)
    prod = jnp.concatenate([s_re * f_re - s_im * f_im, s_re * f_im + s_im * f_re], axis=0)
    time = dot(inv, prod.astype(jnp.bfloat16), ((1,), (0,)))
    c_re, c_im = time[:lanes], time[lanes:]
    d = jnp.concatenate([c_re * cos + c_im * sin, c_im * cos - c_re * sin], axis=1)
    long_out = dot(edge, d.astype(jnp.bfloat16), ((1,), (1,))) * (1.0 / (size * lanes))
    both = long_out + param(9) * mixed.astype(jnp.float32)
    out_ref[...] = jnp.where(lane < 2, back(conv, 4) * both, both)


def pack(proj, filter_spectrum, taps, skip, gain):
    chans, lanes = proj.shape[1], proj.shape[2]
    hbm = pl.BlockSpec(memory_space=pltpu.HBM)
    vmem = pl.BlockSpec(memory_space=pltpu.VMEM)
    inputs = (proj, filter_spectrum, taps, skip, gain)
    return pl.pallas_call(
        pack_kernel,
        out_shape=(
            jax.ShapeDtypeStruct((chans * ROWS, lanes), jnp.bfloat16),
            jax.ShapeDtypeStruct((chans, lanes), jnp.float32),
        ),
        in_specs=[hbm] * len(inputs),
        out_specs=(vmem, vmem),
        scratch_shapes=[
            pltpu.VMEM(proj.shape, proj.dtype),
            pltpu.VMEM(filter_spectrum.shape, filter_spectrum.dtype),
            pltpu.VMEM((16, lanes), jnp.float32),
            pltpu.VMEM((chans * ROWS, lanes), jnp.float32),
            pltpu.SemaphoreType.DMA((2, CHUNKS)),
            pltpu.SemaphoreType.DMA((5,)),
        ],
        compiler_params=pltpu.CompilerParams(vmem_limit_bytes=16 * 2**20),
    )(*(pltpu.with_memory_space_constraint(x, pltpu.HBM) for x in inputs))


def convolve(recv, waves):
    lanes = recv.shape[1]
    shards = recv.shape[0] // ROWS
    vmem = pl.BlockSpec(memory_space=pltpu.VMEM)
    return pl.pallas_call(
        channel_kernel,
        out_shape=(jax.ShapeDtypeStruct((shards, lanes), jnp.float32),) * 2,
        in_specs=[vmem] * 2,
        out_specs=(vmem,) * 2,
        scratch_shapes=[pltpu.VMEM((shards * ROWS, lanes), jnp.float32)],
        compiler_params=pltpu.CompilerParams(vmem_limit_bytes=16 * 2**20),
    )(recv, waves)


def per_device(proj, short_filter, skip_gain, norm_gain, filter_spectrum):
    chans, tok = proj.shape[1], proj.shape[2]
    peers = lax.axis_size("seq")
    groups = lax.axis_size("tp")
    waves = tables(peers, tok)
    taps = jnp.swapaxes(short_filter, 1, 2)
    sent, factor = pack(proj, filter_spectrum, taps, skip_gain[None], norm_gain[None])
    recv = lax.all_to_all(
        sent.reshape(peers, ROWS // 2, 2, tok), "seq", split_axis=0, concat_axis=0, tiled=True
    )
    part, gain = convolve(recv.reshape(peers * ROWS, tok), waves)
    part = lax.all_to_all(
        part.reshape(peers, 1, tok), "seq", split_axis=0, concat_axis=0, tiled=True
    )
    pre = part.reshape(chans, tok) * factor
    squares = jnp.broadcast_to(jnp.sum(pre * pre, axis=0)[None, None], (groups, 1, tok))
    squares = lax.all_to_all(squares, "tp", split_axis=0, concat_axis=0, tiled=True)
    meansq = jnp.sum(squares[:, 0], axis=0) / (chans * groups)
    return (pre * lax.rsqrt(meansq + 1e-05)[None, :] * gain).astype(jnp.bfloat16)


def solution(mesh):
    return jax.shard_map(
        per_device,
        mesh=mesh,
        in_specs=(
            P(None, "tp", "seq"),
            P(None, "tp", None),
            P("tp"),
            P("tp"),
            P(None, "tp", "seq"),
        ),
        out_specs=P("tp", "seq"),
        check_vma=False,
    )
```

time: 61.7 us -> 60.6 us (0.982)
  blocking collectives: 58.5 us -> 57.1 us
    all_to_all x2, blocking collectives: 50.6 us -> 49.2 us  [the longest x1 31.7 us: per_device(): lax.all_to_all(sent.reshape(peers, ROWS // 2, 2, tok), 'seq', split_axis=...]
where the time goes in v4:
time: 60.6 us; the launch traced here: 60.4 us
  blocking collectives  57.1 us (94%)
  Pallas kernels  2.58 us (4%)
  other arithmetic  0.69 us (1%)
    all_to_all x1, blocking collectives, per_device(): lax.all_to_all(sent.reshape(peers, ROWS // 2, 2, tok), 'seq', split_axis=...  31.7 us
    all_to_all x1, blocking collectives, per_device(): lax.all_to_all(part.reshape(peers, 1, tok), 'seq', split_axis=0, concat_a...  17.5 us
    all_to_all x1, blocking collectives, per_device(): lax.all_to_all(squares, 'tp', split_axis=0, concat_axis=0, tiled=True)  7.92 us
    pallas_call x1, Pallas kernels, pack(): pl.pallas_call(pack_kernel, out_shape=(jax.ShapeDtypeStruct((chans * ROWS...  1.54 us

profile of v4, /device:TPU:1, one launch (start us, length us, event | category | flops | bytes accessed | tf_op | source)
XLA Modules:
  0.0 60.4 jit_solution(14659855276501053177)
XLA Ops:
  0.0 1.5 %shard_map.64 = (bf16[768,128]{1,0:T(8,128)(2,1)S(1)}, f32[128,128]{1,0:T(8,128)S(1)}) custom-call(bf16[3,128,128]{2,1,0:T(8,128)(2,1)} %proj_hbm.1, f32[2,128,256]{2,1,0:T(8,128)} %filt_hbm.1, f32[3,3,128]{2,1,0:T(4,128)} %bitcast.15, f32[1,128]{1,0:T(1,128)} %bitcast.16, f32[1,128]{1,0:T(1,128)} %bitcast.17), custom_call_target="tpu_custom_call" | custom-call | tf_op jit(solution)/shard_map/pallas_call | solution.py:167
  1.5 0.0 copy-start
  1.6 31.7 %all_to_all.15 = bf16[128,3,2,128]{3,2,1,0:T(2,128)(2,1)S(1)} all-to-all(bf16[128,3,2,128]{3,2,1,0:T(2,128)(2,1)S(1)} %bitcast.11), channel_id=1, replica_groups=mesh['seq'=128,'tp'=4] {'seq'}, dimensions={0} | all-to-all | bytes 393216 | tf_op jit(solution)/shard_map/all_to_all | solution.py:208
  33.3 0.0 copy-done
  33.3 1.0 %shard_map.65 = (f32[128,128]{1,0:T(8,128)S(1)}, f32[128,128]{1,0:T(8,128)S(1)}) custom-call(bf16[768,128]{1,0:T(8,128)(2,1)S(1)} %bitcast.10, bf16[256,512]{1,0:T(8,128)(2,1)S(1)} %copy-done), custom_call_target="tpu_custom_call" | custom-call | tf_op jit(solution)/shard_map/pallas_call | solution.py:191
  34.3 17.5 %all_to_all.16 = f32[128,1,128]{2,1,0:T(1,128)S(1)} all-to-all(f32[128,1,128]{2,1,0:T(1,128)S(1)} %bitcast.12), channel_id=1, replica_groups=mesh['seq'=128,'tp'=4] {'seq'}, dimensions={0} | all-to-all | bytes 131072 | tf_op jit(solution)/shard_map/all_to_all | solution.py:212
  51.8 7.9 %all_to_all.17 = f32[4,1,128]{2,1,0:T(1,128)S(1)} all-to-all(f32[4,1,128]{2,1,0:T(1,128)S(1)} %broadcast_in_dim.15), channel_id=1, replica_groups=mesh['seq'=128,'tp'=4] {'tp'}, dimensions={0} | all-to-all | bytes 4096 | tf_op jit(solution)/shard_map/all_to_all | solution.py:217
  59.8 0.6 %multiply_convert_fusion = bf16[128,128]{1,0:T(8,128)(2,1)} fusion(f32[128,128]{1,0:T(8,128)S(1)} %get-tuple-element.12, f32[128,128]{1,0:T(8,128)S(1)} %get-tuple-element.14, f32[128]{0:T(128)S(1)} %add_rsqrt_fusion), kind=kLoop, calls=%fused_computation | loop fusion | flops 49152 | bytes 164352 | tf_op jit(solution)/shard_map/convert_element_type | solution.py:219
  (4 shorter events, 0.1 us)
Async XLA Ops:
  1.5 31.7 %copy-start = (bf16[256,512]{1,0:T(8,128)(2,1)S(1)}, bf16[256,512]{1,0:T(8,128)(2,1)}, u32[]{:S(2)}) copy-start(bf16[256,512]{1,0:T(8,128)(2,1)} %constant.9.clone.waves_ref) | copy-start | bytes 786436

commit v5 on v4

v5 whole, which is shorter than its diff:
```python
import jax
import jax.numpy as jnp
import numpy as np
from jax import lax
from jax.experimental import pallas as pl
from jax.experimental.pallas import tpu as pltpu
from jax.sharding import PartitionSpec as P

ROWS = 6
EDGE_ROW = 5
CHUNKS = 1


def tables(n_coarse, n_fine):
    total = 2 * n_coarse * n_fine
    n1 = np.arange(n_coarse)
    k1 = np.arange(2 * n_coarse)
    n2 = np.arange(n_fine)
    turn = 2.0 * np.pi * (np.outer(n2, k1) % total) / total
    first = 2.0 * np.pi * (np.outer(n1, k1[:n_coarse]) % (2 * n_coarse)) / (2 * n_coarse)
    edge = np.concatenate([np.cos(first), -np.sin(first)], axis=1)
    inner = 2.0 * np.pi * (np.outer(n2, n2) % n_fine) / n_fine
    inner = np.concatenate([np.cos(inner), -np.sin(inner)], axis=1)
    fold = lambda x: np.concatenate([x[: len(x) // 2], x[len(x) // 2 :]], axis=1)
    turns = np.concatenate([np.cos(turn), -np.sin(turn)], axis=1)
    rows = [fold(edge), fold(inner), turns]
    return jnp.asarray(np.concatenate(rows, axis=0), jnp.bfloat16)


def pack_kernel(
    proj_hbm, filt_hbm, taps_hbm, skip_hbm, gain_hbm,
    out_ref, query_ref, columns_ref, own_ref,
    proj_ref, filt_ref, taps_ref, small_ref, wide, sem_in, sem_small
):
    chans = proj_ref.shape[1]
    lanes = proj_ref.shape[2]
    size = chans // CHUNKS
    small = [
        pltpu.make_async_copy(taps_hbm, taps_ref, sem_small.at[0]),
        pltpu.make_async_copy(skip_hbm, small_ref.at[pl.ds(9, 1)], sem_small.at[1]),
        pltpu.make_async_copy(gain_hbm, small_ref.at[pl.ds(10, 1)], sem_small.at[2]),
    ]
    loads = []
    for chunk in range(CHUNKS):
        part = pl.ds(chunk * size, size)
        loads.append([
            pltpu.make_async_copy(proj_hbm.at[:, part], proj_ref.at[:, part], sem_in.at[0, chunk]),
            pltpu.make_async_copy(filt_hbm.at[:, part], filt_ref.at[:, part], sem_in.at[1, chunk]),
        ])
    for copy in small + sum(loads, []):
        copy.start()
    for copy in small:
        copy.wait()
    for i in range(3):
        small_ref[3 * i : 3 * i + 3, :] = taps_ref[i]
    lane = lax.broadcasted_iota(jnp.int32, (16, lanes), 1)
    param = lax.broadcasted_iota(jnp.int32, (16, lanes), 0)
    params = jnp.where(param < 11, small_ref[...], 0.0)
    columns = params.T
    columns_ref[...] = columns
    mine = jnp.where(lane == lax.axis_index("seq"), params, 0.0)
    own_ref[...] = jnp.broadcast_to(jnp.sum(mine, axis=1, keepdims=True), (16, lanes))
    lane = lax.broadcasted_iota(jnp.int32, (size, lanes), 1)
    for chunk in range(CHUNKS):
        for copy in loads[chunk]:
            copy.wait()
        base = chunk * size
        rows = pl.ds(base * ROWS, size * ROWS)
        row = lambda r: pl.ds(base * ROWS + r, size, stride=ROWS)
        raw = [proj_ref[i, base : base + size].astype(jnp.float32) for i in range(3)]

        twice = [None] + [pltpu.roll(x, 2, 1) for x in raw[1:]]

        def conv(i):
            tap = lambda m: columns[base : base + size, 3 * i + m : 3 * i + m + 1]
            late = tap(1) * jnp.where(lane < 1, 0.0, pltpu.roll(raw[i], 1, 1))
            return tap(0) * raw[i] + late + tap(2) * jnp.where(lane < 2, 0.0, twice[i])

        query_ref[base : base + size, :] = proj_ref[0, base : base + size]
        wide[row(0), :] = conv(1) * conv(2)
        for part in range(2):
            for half in range(2):
                wide[row(1 + 2 * part + half), :] = filt_ref[
                    part, base : base + size, lanes * half : lanes * (half + 1)
                ]
        fourth = pltpu.roll(raw[0], 4, 1)
        heads = jnp.where(lane < 2, raw[1], jnp.where(lane < 4, twice[2], fourth))
        tails = jnp.where(lane < 2, twice[2], jnp.where(lane < 4, fourth, raw[1]))
        edges = jnp.where(lane < 8, heads, pltpu.roll(tails, 10, 1))
        wide[row(EDGE_ROW), :] = edges
        out_ref[rows, :] = wide[rows, :].astype(jnp.bfloat16)


def channel_kernel(
    recv_ref, query_ref, columns_ref, own_ref, waves_ref, out_ref, factor_ref, gain_ref, wide
):
    shards = out_ref.shape[0]
    lanes = out_ref.shape[1]
    size = 2 * shards
    wide[...] = recv_ref[...].astype(jnp.float32)
    plane = lambda r: wide[pl.ds(r, shards, stride=ROWS), :]
    lane = lax.broadcasted_iota(jnp.int32, (shards, lanes), 1)
    shard = lax.broadcasted_iota(jnp.int32, (shards, lanes), 0)

    edges = plane(EDGE_ROW).T
    at = lax.broadcasted_iota(jnp.int32, (8, shards), 0)
    column = lax.broadcasted_iota(jnp.int32, (8, shards), 1)
    own = lambda p: own_ref[p : p + 1, :]
    tap = lambda m: jnp.where(at < 2, own(3 + m), jnp.where(at < 4, own(6 + m), own(m)))
    heads = edges[:8]
    two_ago = jnp.where(column == 0, 0.0, pltpu.roll(edges[8:16], 1, 1))
    one_ago = jnp.where(at % 2 == 1, pltpu.roll(heads, 1, 0), pltpu.roll(two_ago, 7, 0))
    conv = tap(0) * heads + tap(1) * one_ago + tap(2) * two_ago
    repair = (conv * pltpu.roll(conv, 6, 0)).astype(jnp.bfloat16).astype(jnp.float32)
    upright = plane(0).T
    mixed = jnp.concatenate([jnp.where(at < 2, repair, upright[:8]), upright[8:]], axis=0)
    rest = jnp.zeros((lanes - 8, shards), jnp.float32)
    spread = lambda x: jnp.concatenate([x, rest], axis=0).T
    skipped = own(9) * jnp.where(lane < 2, spread(repair), plane(0))
    query = spread(pltpu.roll(conv, 4, 0))

    unfold = lambda x: jnp.concatenate([x[:, :size], x[:, size:]], axis=0)
    square = lambda a, b, c, d: jnp.concatenate(
        [jnp.concatenate([a, b], axis=1), jnp.concatenate([c, d], axis=1)], axis=0
    )
    dot = lambda a, b, dims: lax.dot_general(
        a, b, (dims, ((), ())), preferred_element_type=jnp.float32
    )
    half = shards // 2
    edge = unfold(waves_ref[:half, :])
    flip = jnp.where(shard % 2 == 0, 1.0, -1.0).astype(jnp.bfloat16)
    c, d = edge[:, :shards], edge[:, shards:]
    edge = jnp.concatenate([c, c * flip, d, d * flip], axis=1)
    inner = unfold(waves_ref[half : half + lanes // 2, :])
    w_re, w_im = inner[:, :lanes], inner[:, lanes:]
    fwd, inv = square(w_re, -w_im, w_im, w_re), square(w_re, w_im, -w_im, w_re)
    turns = waves_ref[half + lanes // 2 :, :].astype(jnp.float32)
    cos, sin = turns[:, :size], turns[:, size:]

    part = dot(mixed.astype(jnp.bfloat16), edge, ((1,), (0,)))
    a_re, a_im = part[:, :size], part[:, size:]
    b = jnp.concatenate([a_re * cos - a_im * sin, a_re * sin + a_im * cos], axis=0)
    spec = dot(fwd, b.astype(jnp.bfloat16), ((1,), (0,)))
    s_re, s_im = spec[:lanes], spec[lanes:]
    f_re = jnp.concatenate([plane(1), plane(2)], axis=1)
    f_im = jnp.concatenate([plane(3), plane(4)], axis=1)
    prod = jnp.concatenate([s_re * f_re - s_im * f_im, s_re * f_im + s_im * f_re], axis=0)
    time = dot(inv, prod.astype(jnp.bfloat16), ((1,), (0,)))
    c_re, c_im = time[:lanes], time[lanes:]
    d = jnp.concatenate([c_re * cos + c_im * sin, c_im * cos - c_re * sin], axis=1)
    long_out = dot(edge, d.astype(jnp.bfloat16), ((1,), (1,))) * (1.0 / (size * lanes))
    raw = query_ref[...].astype(jnp.float32)
    weight = lambda p: columns_ref[:, p : p + 1]
    gain_ref[...] = jnp.broadcast_to(weight(10), (shards, lanes))
    late = weight(1) * jnp.where(lane < 1, 0.0, pltpu.roll(raw, 1, 1))
    late = weight(0) * raw + late + weight(2) * jnp.where(lane < 2, 0.0, pltpu.roll(raw, 2, 1))
    factor_ref[...] = jnp.where(lane < 2, 1.0, late)
    both = long_out + skipped
    out_ref[...] = jnp.where(lane < 2, query * both, both)


def pack(proj, filter_spectrum, taps, skip, gain):
    chans, lanes = proj.shape[1], proj.shape[2]
    hbm = pl.BlockSpec(memory_space=pltpu.HBM)
    vmem = pl.BlockSpec(memory_space=pltpu.VMEM)
    inputs = (proj, filter_spectrum, taps, skip, gain)
    return pl.pallas_call(
        pack_kernel,
        out_shape=(
            jax.ShapeDtypeStruct((chans * ROWS, lanes), jnp.bfloat16),
            jax.ShapeDtypeStruct((chans, lanes), jnp.bfloat16),
            jax.ShapeDtypeStruct((chans, 16), jnp.float32),
            jax.ShapeDtypeStruct((16, lanes), jnp.float32),
        ),
        in_specs=[hbm] * len(inputs),
        out_specs=(vmem,) * 4,
        scratch_shapes=[
            pltpu.VMEM(proj.shape, proj.dtype),
            pltpu.VMEM(filter_spectrum.shape, filter_spectrum.dtype),
            pltpu.VMEM(taps.shape, taps.dtype),
            pltpu.VMEM((16, lanes), jnp.float32),
            pltpu.VMEM((chans * ROWS, lanes), jnp.float32),
            pltpu.SemaphoreType.DMA((2, CHUNKS)),
            pltpu.SemaphoreType.DMA((3,)),
        ],
        compiler_params=pltpu.CompilerParams(vmem_limit_bytes=16 * 2**20),
    )(*(pltpu.with_memory_space_constraint(x, pltpu.HBM) for x in inputs))


def convolve(recv, query, columns, own, waves):
    lanes = recv.shape[1]
    shards = recv.shape[0] // ROWS
    vmem = pl.BlockSpec(memory_space=pltpu.VMEM)
    return pl.pallas_call(
        channel_kernel,
        out_shape=(jax.ShapeDtypeStruct((shards, lanes), jnp.float32),) * 3,
        in_specs=[vmem] * 5,
        out_specs=(vmem,) * 3,
        scratch_shapes=[pltpu.VMEM((shards * ROWS, lanes), jnp.float32)],
        compiler_params=pltpu.CompilerParams(vmem_limit_bytes=16 * 2**20),
    )(recv, query, columns, own, waves)


def per_device(proj, short_filter, skip_gain, norm_gain, filter_spectrum):
    chans, tok = proj.shape[1], proj.shape[2]
    peers = lax.axis_size("seq")
    groups = lax.axis_size("tp")
    waves = tables(peers, tok)
    taps = jnp.swapaxes(short_filter, 1, 2)
    sent, query, columns, own = pack(proj, filter_spectrum, taps, skip_gain[None], norm_gain[None])
    recv = lax.all_to_all(
        sent.reshape(peers, ROWS // 2, 2, tok), "seq", split_axis=0, concat_axis=0, tiled=True
    )
    recv = recv.reshape(peers * ROWS, tok)
    part, factor, gain = convolve(recv, query, columns, own, waves)
    part = lax.all_to_all(
        part.reshape(peers, 1, tok), "seq", split_axis=0, concat_axis=0, tiled=True
    )
    pre = part.reshape(chans, tok) * factor
    squares = lax.all_gather(jnp.sum(pre * pre, axis=0)[None], "tp", axis=0, tiled=True)
    meansq = jnp.sum(squares, axis=0) / (chans * groups)
    return (pre * lax.rsqrt(meansq + 1e-05)[None, :] * gain).astype(jnp.bfloat16)


def solution(mesh):
    return jax.shard_map(
        per_device,
        mesh=mesh,
        in_specs=(
            P(None, "tp", "seq"),
            P(None, "tp", None),
            P("tp"),
            P("tp"),
            P(None, "tp", "seq"),
        ),
        out_specs=P("tp", "seq"),
        check_vma=False,
    )
```

time: 60.6 us -> 60.3 us (level)
    all_to_all x1 -> x0, blocking collectives: 7.92 us -> none  [per_device(): lax.all_to_all(squares, 'tp', split_axis=0, concat_axis=0, tiled=True)]
    all_gather x0 -> x1, blocking collectives: none -> 7.64 us  [per_device(): lax.all_gather(jnp.sum(pre * pre, axis=0)[None], 'tp', axis=0, tiled=True)]
where the time goes in v5:
time: 60.3 us; the launch traced here: 59.8 us
  blocking collectives  56.8 us (94%)
  Pallas kernels  2.28 us (4%)
  other arithmetic  0.7 us (1%)
    all_to_all x1, blocking collectives, per_device(): lax.all_to_all(sent.reshape(peers, ROWS // 2, 2, tok), 'seq', split_axis=...  31.7 us
    all_to_all x1, blocking collectives, per_device(): lax.all_to_all(part.reshape(peers, 1, tok), 'seq', split_axis=0, concat_a...  17.5 us
    all_gather x1, blocking collectives, per_device(): lax.all_gather(jnp.sum(pre * pre, axis=0)[None], 'tp', axis=0, tiled=True)  7.64 us
    pallas_call x1, Pallas kernels, pack(): pl.pallas_call(pack_kernel, out_shape=(jax.ShapeDtypeStruct((chans * ROWS...  1.38 us

profile of v5, /device:TPU:1, one launch (start us, length us, event | category | flops | bytes accessed | tf_op | source)
XLA Modules:
  0.0 59.8 jit_solution(3214558997190563853)
XLA Ops:
  0.0 1.4 %shard_map.64 = (bf16[768,128]{1,0:T(8,128)(2,1)S(1)}, bf16[128,128]{1,0:T(8,128)(2,1)S(1)}, f32[128,16]{1,0:T(8,128)S(1)}, f32[16,128]{1,0:T(8,128)S(1)}) custom-call(bf16[3,128,128]{2,1,0:T(8,128)(2,1)} %proj_hbm.1, f32[2,128,256]{2,1,0:T(8,128)} %filt_hbm.1, f32[3,3,128]{2,1,0:T(4,128)} %bitcast.14, f32[1,128]{1,0:T(1,128)} %bitcast.16, f32[1,128]{1,0:T(1,128)} %bitcast.17), custom_call_target="tpu_custom_call" | custom-call | tf_op jit(solution)/shard_map/pallas_call | solution.py:167
  1.4 0.0 copy-start
  1.4 31.7 %all_to_all.10 = bf16[128,3,2,128]{3,2,1,0:T(2,128)(2,1)S(1)} all-to-all(bf16[128,3,2,128]{3,2,1,0:T(2,128)(2,1)S(1)} %bitcast.11), channel_id=1, replica_groups=mesh['seq'=128,'tp'=4] {'seq'}, dimensions={0} | all-to-all | bytes 393216 | tf_op jit(solution)/shard_map/all_to_all | solution.py:211
  33.1 0.0 copy-done
  33.1 0.9 %shard_map.65 = (f32[128,128]{1,0:T(8,128)S(1)}, f32[128,128]{1,0:T(8,128)S(1)}, f32[128,128]{1,0:T(8,128)S(1)}) custom-call(bf16[768,128]{1,0:T(8,128)(2,1)S(1)} %bitcast.10, bf16[128,128]{1,0:T(8,128)(2,1)S(1)} %get-tuple-element.13.query_ref, f32[128,16]{1,0:T(8,128)S(1)} %get-tuple-element.14.columns_ref, f32[16,128]{1,0:T(8,128)S(1)} %get-tuple-element.15.own_ref, ...), custom_call_target="tpu_custom_call" | custom-call | tf_op jit(solution)/shard_map/pallas_call | solution.py:194
  34.0 17.5 %all_to_all.11 = f32[128,1,128]{2,1,0:T(1,128)S(1)} all-to-all(f32[128,1,128]{2,1,0:T(1,128)S(1)} %bitcast.12), channel_id=1, replica_groups=mesh['seq'=128,'tp'=4] {'seq'}, dimensions={0} | all-to-all | bytes 131072 | tf_op jit(solution)/shard_map/all_to_all | solution.py:216
  51.5 7.6 %all-gather.1 = f32[4,1,128]{2,1,0:T(1,128)S(1)} all-gather(f32[1,1,128]{2,1,0:T(1,128)S(1)} %bitcast.15), channel_id=2, replica_groups=mesh['seq'=128,'tp'=4] {'tp'}, dimensions={0}, use_global_device_ids=true | all-gather | bytes 2560 | tf_op jit(solution)/shard_map/all_gather | solution.py:220
  59.2 0.6 %multiply_convert_fusion = bf16[128,128]{1,0:T(8,128)(2,1)} fusion(f32[128,128]{1,0:T(8,128)S(1)} %get-tuple-element.18, f32[128,128]{1,0:T(8,128)S(1)} %get-tuple-element.20, f32[128]{0:T(128)S(1)} %add_rsqrt_fusion), kind=kLoop, calls=%fused_computation | loop fusion | flops 49152 | bytes 164352 | tf_op jit(solution)/shard_map/convert_element_type | solution.py:222
  (3 shorter events, 0.1 us)
Async XLA Ops:
  1.4 31.7 %copy-start = (bf16[256,512]{1,0:T(8,128)(2,1)S(1)}, bf16[256,512]{1,0:T(8,128)(2,1)}, u32[]{:S(2)}) copy-start(bf16[256,512]{1,0:T(8,128)(2,1)} %constant.9.clone.waves_ref) | copy-start | bytes 786436

commit v6 on v5

--- a/solution.py
+++ b/solution.py
@@ -8,7 +8,6 @@
 
 ROWS = 6
 EDGE_ROW = 5
-CHUNKS = 1
 
 
 def tables(n_coarse, n_fine):
@@ -34,20 +33,20 @@
 ):
     chans = proj_ref.shape[1]
     lanes = proj_ref.shape[2]
-    size = chans // CHUNKS
     small = [
         pltpu.make_async_copy(taps_hbm, taps_ref, sem_small.at[0]),
         pltpu.make_async_copy(skip_hbm, small_ref.at[pl.ds(9, 1)], sem_small.at[1]),
         pltpu.make_async_copy(gain_hbm, small_ref.at[pl.ds(10, 1)], sem_small.at[2]),
     ]
-    loads = []
-    for chunk in range(CHUNKS):
-        part = pl.ds(chunk * size, size)
-        loads.append([
-            pltpu.make_async_copy(proj_hbm.at[:, part], proj_ref.at[:, part], sem_in.at[0, chunk]),
-            pltpu.make_async_copy(filt_hbm.at[:, part], filt_ref.at[:, part], sem_in.at[1, chunk]),
-        ])
-    for copy in small + sum(loads, []):
+    proj_loads = [
+        pltpu.make_async_copy(proj_hbm.at[:], proj_ref.at[:], sem_in.at[0, k])
+        for k in range(1)
+    ]
+    filt_loads = [
+        pltpu.make_async_copy(filt_hbm.at[k], filt_ref.at[k], sem_in.at[1, k])
+        for k in range(2)
+    ]
+    for copy in small + proj_loads + filt_loads:
         copy.start()
     for copy in small:
         copy.wait()
@@ -60,35 +59,32 @@
     columns_ref[...] = columns
     mine = jnp.where(lane == lax.axis_index("seq"), params, 0.0)
     own_ref[...] = jnp.broadcast_to(jnp.sum(mine, axis=1, keepdims=True), (16, lanes))
-    lane = lax.broadcasted_iota(jnp.int32, (size, lanes), 1)
-    for chunk in range(CHUNKS):
-        for copy in loads[chunk]:
-            copy.wait()
-        base = chunk * size
-        rows = pl.ds(base * ROWS, size * ROWS)
-        row = lambda r: pl.ds(base * ROWS + r, size, stride=ROWS)
-        raw = [proj_ref[i, base : base + size].astype(jnp.float32) for i in range(3)]
-
-        twice = [None] + [pltpu.roll(x, 2, 1) for x in raw[1:]]
-
-        def conv(i):
-            tap = lambda m: columns[base : base + size, 3 * i + m : 3 * i + m + 1]
-            late = tap(1) * jnp.where(lane < 1, 0.0, pltpu.roll(raw[i], 1, 1))
-            return tap(0) * raw[i] + late + tap(2) * jnp.where(lane < 2, 0.0, twice[i])
-
-        query_ref[base : base + size, :] = proj_ref[0, base : base + size]
-        wide[row(0), :] = conv(1) * conv(2)
-        for part in range(2):
-            for half in range(2):
-                wide[row(1 + 2 * part + half), :] = filt_ref[
-                    part, base : base + size, lanes * half : lanes * (half + 1)
-                ]
-        fourth = pltpu.roll(raw[0], 4, 1)
-        heads = jnp.where(lane < 2, raw[1], jnp.where(lane < 4, twice[2], fourth))
-        tails = jnp.where(lane < 2, twice[2], jnp.where(lane < 4, fourth, raw[1]))
-        edges = jnp.where(lane < 8, heads, pltpu.roll(tails, 10, 1))
-        wide[row(EDGE_ROW), :] = edges
-        out_ref[rows, :] = wide[rows, :].astype(jnp.bfloat16)
+    lane = lax.broadcasted_iota(jnp.int32, (chans, lanes), 1)
+    row = lambda r: pl.ds(r, chans, stride=ROWS)
+    for copy in proj_loads:
+        copy.wait()
+    raw = [proj_ref[i].astype(jnp.float32) for i in range(3)]
+    twice = [None] + [pltpu.roll(x, 2, 1) for x in raw[1:]]
+
+    def conv(i):
+        tap = lambda m: columns[:, 3 * i + m : 3 * i + m + 1]
+        late = tap(1) * jnp.where(lane < 1, 0.0, pltpu.roll(raw[i], 1, 1))
+        return tap(0) * raw[i] + late + tap(2) * jnp.where(lane < 2, 0.0, twice[i])
+
+    query_ref[...] = proj_ref[0]
+    wide[row(0), :] = conv(1) * conv(2)
+    fourth = pltpu.roll(raw[0], 4, 1)
+    heads = jnp.where(lane < 2, raw[1], jnp.where(lane < 4, twice[2], fourth))
+    tails = jnp.where(lane < 2, twice[2], jnp.where(lane < 4, fourth, raw[1]))
+    wide[row(EDGE_ROW), :] = jnp.where(lane < 8, heads, pltpu.roll(tails, 10, 1))
+    for copy in filt_loads:
+        copy.wait()
+    for part in range(2):
+        for half in range(2):
+            wide[row(1 + 2 * part + half), :] = filt_ref[
+                part, :, lanes * half : lanes * (half + 1)
+            ]
+    out_ref[...] = wide[...].astype(jnp.bfloat16)
 
 
 def channel_kernel(
@@ -180,7 +176,7 @@
             pltpu.VMEM(taps.shape, taps.dtype),
             pltpu.VMEM((16, lanes), jnp.float32),
             pltpu.VMEM((chans * ROWS, lanes), jnp.float32),
-            pltpu.SemaphoreType.DMA((2, CHUNKS)),
+            pltpu.SemaphoreType.DMA((2, 4)),
             pltpu.SemaphoreType.DMA((3,)),
         ],
         compiler_params=pltpu.CompilerParams(vmem_limit_bytes=16 * 2**20),

time: 60.3 us -> 60.2 us (level)
  no operation moved by 1% of the time
where the time goes in v6:
time: 60.2 us; the launch traced here: 59.8 us
  blocking collectives  56.8 us (94%)
  Pallas kernels  2.23 us (4%)
  other arithmetic  0.7 us (1%)
    all_to_all x1, blocking collectives, per_device(): lax.all_to_all(sent.reshape(peers, ROWS // 2, 2, tok), 'seq', split_axis=...  31.7 us
    all_to_all x1, blocking collectives, per_device(): lax.all_to_all(part.reshape(peers, 1, tok), 'seq', split_axis=0, concat_a...  17.5 us
    all_gather x1, blocking collectives, per_device(): lax.all_gather(jnp.sum(pre * pre, axis=0)[None], 'tp', axis=0, tiled=True)  7.63 us
    pallas_call x1, Pallas kernels, pack(): pl.pallas_call(pack_kernel, out_shape=(jax.ShapeDtypeStruct((chans * ROWS...  1.32 us

profile of v6, /device:TPU:1, one launch (start us, length us, event | category | flops | bytes accessed | tf_op | source)
XLA Modules:
  0.0 59.8 jit_solution(7850916866356242667)
XLA Ops:
  0.0 1.3 %shard_map.64 = (bf16[768,128]{1,0:T(8,128)(2,1)S(1)}, bf16[128,128]{1,0:T(8,128)(2,1)S(1)}, f32[128,16]{1,0:T(8,128)S(1)}, f32[16,128]{1,0:T(8,128)S(1)}) custom-call(bf16[3,128,128]{2,1,0:T(8,128)(2,1)} %proj_hbm.1, f32[2,128,256]{2,1,0:T(8,128)} %filt_hbm.1, f32[3,3,128]{2,1,0:T(4,128)} %bitcast.14, f32[1,128]{1,0:T(1,128)} %bitcast.16, f32[1,128]{1,0:T(1,128)} %bitcast.17), custom_call_target="tpu_custom_call" | custom-call | tf_op jit(solution)/shard_map/pallas_call | solution.py:163
  1.3 0.0 copy-start
  1.3 31.7 %all_to_all.10 = bf16[128,3,2,128]{3,2,1,0:T(2,128)(2,1)S(1)} all-to-all(bf16[128,3,2,128]{3,2,1,0:T(2,128)(2,1)S(1)} %bitcast.11), channel_id=1, replica_groups=mesh['seq'=128,'tp'=4] {'seq'}, dimensions={0} | all-to-all | bytes 393216 | tf_op jit(solution)/shard_map/all_to_all | solution.py:207
  33.1 0.0 copy-done
  33.1 0.9 %shard_map.65 = (f32[128,128]{1,0:T(8,128)S(1)}, f32[128,128]{1,0:T(8,128)S(1)}, f32[128,128]{1,0:T(8,128)S(1)}) custom-call(bf16[768,128]{1,0:T(8,128)(2,1)S(1)} %bitcast.10, bf16[128,128]{1,0:T(8,128)(2,1)S(1)} %get-tuple-element.13.query_ref, f32[128,16]{1,0:T(8,128)S(1)} %get-tuple-element.14.columns_ref, f32[16,128]{1,0:T(8,128)S(1)} %get-tuple-element.15.own_ref, ...), custom_call_target="tpu_custom_call" | custom-call | tf_op jit(solution)/shard_map/pallas_call | solution.py:190
  34.0 17.5 %all_to_all.11 = f32[128,1,128]{2,1,0:T(1,128)S(1)} all-to-all(f32[128,1,128]{2,1,0:T(1,128)S(1)} %bitcast.12), channel_id=1, replica_groups=mesh['seq'=128,'tp'=4] {'seq'}, dimensions={0} | all-to-all | bytes 131072 | tf_op jit(solution)/shard_map/all_to_all | solution.py:212
  51.5 7.6 %all-gather.1 = f32[4,1,128]{2,1,0:T(1,128)S(1)} all-gather(f32[1,1,128]{2,1,0:T(1,128)S(1)} %bitcast.15), channel_id=2, replica_groups=mesh['seq'=128,'tp'=4] {'tp'}, dimensions={0}, use_global_device_ids=true | all-gather | bytes 2560 | tf_op jit(solution)/shard_map/all_gather | solution.py:216
  59.2 0.6 %multiply_convert_fusion = bf16[128,128]{1,0:T(8,128)(2,1)} fusion(f32[128,128]{1,0:T(8,128)S(1)} %get-tuple-element.18, f32[128,128]{1,0:T(8,128)S(1)} %get-tuple-element.20, f32[128]{0:T(128)S(1)} %add_rsqrt_fusion), kind=kLoop, calls=%fused_computation | loop fusion | flops 49152 | bytes 164352 | tf_op jit(solution)/shard_map/convert_element_type | solution.py:218
  (3 shorter events, 0.1 us)
Async XLA Ops:
  1.3 31.7 %copy-start = (bf16[256,512]{1,0:T(8,128)(2,1)S(1)}, bf16[256,512]{1,0:T(8,128)(2,1)}, u32[]{:S(2)}) copy-start(bf16[256,512]{1,0:T(8,128)(2,1)} %constant.9.clone.waves_ref) | copy-start | bytes 786436

commit v7 on v6

--- a/solution.py
+++ b/solution.py
@@ -8,6 +8,7 @@
 
 ROWS = 6
 EDGE_ROW = 5
+SPARE = 16
 
 
 def tables(n_coarse, n_fine):
@@ -34,7 +35,7 @@
     chans = proj_ref.shape[1]
     lanes = proj_ref.shape[2]
     small = [
-        pltpu.make_async_copy(taps_hbm, taps_ref, sem_small.at[0]),
+        pltpu.make_async_copy(taps_hbm, taps_ref.at[pl.ds(0, 3)], sem_small.at[0]),
         pltpu.make_async_copy(skip_hbm, small_ref.at[pl.ds(9, 1)], sem_small.at[1]),
         pltpu.make_async_copy(gain_hbm, small_ref.at[pl.ds(10, 1)], sem_small.at[2]),
     ]
@@ -84,7 +85,7 @@
             wide[row(1 + 2 * part + half), :] = filt_ref[
                 part, :, lanes * half : lanes * (half + 1)
             ]
-    out_ref[...] = wide[...].astype(jnp.bfloat16)
+    out_ref[...] = wide[: chans * ROWS, :].astype(jnp.bfloat16)
 
 
 def channel_kernel(
@@ -93,7 +94,7 @@
     shards = out_ref.shape[0]
     lanes = out_ref.shape[1]
     size = 2 * shards
-    wide[...] = recv_ref[...].astype(jnp.float32)
+    wide[: shards * ROWS, :] = recv_ref[...].astype(jnp.float32)
     plane = lambda r: wide[pl.ds(r, shards, stride=ROWS), :]
     lane = lax.broadcasted_iota(jnp.int32, (shards, lanes), 1)
     shard = lax.broadcasted_iota(jnp.int32, (shards, lanes), 0)
@@ -173,9 +174,9 @@
         scratch_shapes=[
             pltpu.VMEM(proj.shape, proj.dtype),
             pltpu.VMEM(filter_spectrum.shape, filter_spectrum.dtype),
-            pltpu.VMEM(taps.shape, taps.dtype),
+            pltpu.VMEM((6,) + taps.shape[1:], taps.dtype),
             pltpu.VMEM((16, lanes), jnp.float32),
-            pltpu.VMEM((chans * ROWS, lanes), jnp.float32),
+            pltpu.VMEM((chans * ROWS + SPARE, lanes), jnp.float32),
             pltpu.SemaphoreType.DMA((2, 4)),
             pltpu.SemaphoreType.DMA((3,)),
         ],
@@ -192,7 +193,7 @@
         out_shape=(jax.ShapeDtypeStruct((shards, lanes), jnp.float32),) * 3,
         in_specs=[vmem] * 5,
         out_specs=(vmem,) * 3,
-        scratch_shapes=[pltpu.VMEM((shards * ROWS, lanes), jnp.float32)],
+        scratch_shapes=[pltpu.VMEM((shards * ROWS + SPARE, lanes), jnp.float32)],
         compiler_params=pltpu.CompilerParams(vmem_limit_bytes=16 * 2**20),
     )(recv, query, columns, own, waves)
 

time: 60.2 us -> 60.2 us (level)
  no operation moved by 1% of the time
where the time goes in v7:
time: 60.2 us; the launch traced here: 59.8 us
  blocking collectives  56.8 us (94%)
  Pallas kernels  2.23 us (4%)
  other arithmetic  0.7 us (1%)
    all_to_all x1, blocking collectives, per_device(): lax.all_to_all(sent.reshape(peers, ROWS // 2, 2, tok), 'seq', split_axis=...  31.7 us
    all_to_all x1, blocking collectives, per_device(): lax.all_to_all(part.reshape(peers, 1, tok), 'seq', split_axis=0, concat_a...  17.5 us
    all_gather x1, blocking collectives, per_device(): lax.all_gather(jnp.sum(pre * pre, axis=0)[None], 'tp', axis=0, tiled=True)  7.63 us
    pallas_call x1, Pallas kernels, pack(): pl.pallas_call(pack_kernel, out_shape=(jax.ShapeDtypeStruct((chans * ROWS...  1.32 us

profile of v7, /device:TPU:1, one launch (start us, length us, event | category | flops | bytes accessed | tf_op | source)
XLA Modules:
  0.0 59.8 jit_solution(13088411776703077524)
XLA Ops:
  0.0 1.3 %shard_map.64 = (bf16[768,128]{1,0:T(8,128)(2,1)S(1)}, bf16[128,128]{1,0:T(8,128)(2,1)S(1)}, f32[128,16]{1,0:T(8,128)S(1)}, f32[16,128]{1,0:T(8,128)S(1)}) custom-call(bf16[3,128,128]{2,1,0:T(8,128)(2,1)} %proj_hbm.1, f32[2,128,256]{2,1,0:T(8,128)} %filt_hbm.1, f32[3,3,128]{2,1,0:T(4,128)} %bitcast.14, f32[1,128]{1,0:T(1,128)} %bitcast.16, f32[1,128]{1,0:T(1,128)} %bitcast.17), custom_call_target="tpu_custom_call" | custom-call | tf_op jit(solution)/shard_map/pallas_call | solution.py:164
  1.3 0.0 copy-start
  1.3 31.7 %all_to_all.10 = bf16[128,3,2,128]{3,2,1,0:T(2,128)(2,1)S(1)} all-to-all(bf16[128,3,2,128]{3,2,1,0:T(2,128)(2,1)S(1)} %bitcast.11), channel_id=1, replica_groups=mesh['seq'=128,'tp'=4] {'seq'}, dimensions={0} | all-to-all | bytes 393216 | tf_op jit(solution)/shard_map/all_to_all | solution.py:208
  33.1 0.0 copy-done
  33.1 0.9 %shard_map.65 = (f32[128,128]{1,0:T(8,128)S(1)}, f32[128,128]{1,0:T(8,128)S(1)}, f32[128,128]{1,0:T(8,128)S(1)}) custom-call(bf16[768,128]{1,0:T(8,128)(2,1)S(1)} %bitcast.10, bf16[128,128]{1,0:T(8,128)(2,1)S(1)} %get-tuple-element.13.query_ref, f32[128,16]{1,0:T(8,128)S(1)} %get-tuple-element.14.columns_ref, f32[16,128]{1,0:T(8,128)S(1)} %get-tuple-element.15.own_ref, ...), custom_call_target="tpu_custom_call" | custom-call | tf_op jit(solution)/shard_map/pallas_call | solution.py:191
  34.0 17.5 %all_to_all.11 = f32[128,1,128]{2,1,0:T(1,128)S(1)} all-to-all(f32[128,1,128]{2,1,0:T(1,128)S(1)} %bitcast.12), channel_id=1, replica_groups=mesh['seq'=128,'tp'=4] {'seq'}, dimensions={0} | all-to-all | bytes 131072 | tf_op jit(solution)/shard_map/all_to_all | solution.py:213
  51.5 7.6 %all-gather.1 = f32[4,1,128]{2,1,0:T(1,128)S(1)} all-gather(f32[1,1,128]{2,1,0:T(1,128)S(1)} %bitcast.15), channel_id=2, replica_groups=mesh['seq'=128,'tp'=4] {'tp'}, dimensions={0}, use_global_device_ids=true | all-gather | bytes 2560 | tf_op jit(solution)/shard_map/all_gather | solution.py:217
  59.2 0.6 %multiply_convert_fusion = bf16[128,128]{1,0:T(8,128)(2,1)} fusion(f32[128,128]{1,0:T(8,128)S(1)} %get-tuple-element.18, f32[128,128]{1,0:T(8,128)S(1)} %get-tuple-element.20, f32[128]{0:T(128)S(1)} %add_rsqrt_fusion), kind=kLoop, calls=%fused_computation | loop fusion | flops 49152 | bytes 164352 | tf_op jit(solution)/shard_map/convert_element_type | solution.py:219
  (3 shorter events, 0.1 us)
Async XLA Ops:
  1.3 31.7 %copy-start = (bf16[256,512]{1,0:T(8,128)(2,1)S(1)}, bf16[256,512]{1,0:T(8,128)(2,1)}, u32[]{:S(2)}) copy-start(bf16[256,512]{1,0:T(8,128)(2,1)} %constant.9.clone.waves_ref) | copy-start | bytes 786436

commit v8 on v7

--- a/solution.py
+++ b/solution.py
@@ -22,8 +22,8 @@
     inner = 2.0 * np.pi * (np.outer(n2, n2) % n_fine) / n_fine
     inner = np.concatenate([np.cos(inner), -np.sin(inner)], axis=1)
     fold = lambda x: np.concatenate([x[: len(x) // 2], x[len(x) // 2 :]], axis=1)
-    turns = np.concatenate([np.cos(turn), -np.sin(turn)], axis=1)
-    rows = [fold(edge), fold(inner), turns]
+    turns = np.concatenate([np.cos(turn.T), -np.sin(turn.T)], axis=1)
+    rows = [fold(edge), fold(inner), fold(turns), fold(fold(edge.T))]
     return jnp.asarray(np.concatenate(rows, axis=0), jnp.bfloat16)
 
 
@@ -65,18 +65,20 @@
     for copy in proj_loads:
         copy.wait()
     raw = [proj_ref[i].astype(jnp.float32) for i in range(3)]
-    twice = [None] + [pltpu.roll(x, 2, 1) for x in raw[1:]]
+    place = lax.broadcasted_iota(jnp.int32, (lanes, chans), 0)
 
     def conv(i):
-        tap = lambda m: columns[:, 3 * i + m : 3 * i + m + 1]
-        late = tap(1) * jnp.where(lane < 1, 0.0, pltpu.roll(raw[i], 1, 1))
-        return tap(0) * raw[i] + late + tap(2) * jnp.where(lane < 2, 0.0, twice[i])
+        x = raw[i].T
+        tap = lambda m: small_ref[3 * i + m : 3 * i + m + 1, :]
+        late = tap(1) * jnp.where(place < 1, 0.0, pltpu.roll(x, 1, 0))
+        return tap(0) * x + late + tap(2) * jnp.where(place < 2, 0.0, pltpu.roll(x, 2, 0))
 
     query_ref[...] = proj_ref[0]
-    wide[row(0), :] = conv(1) * conv(2)
+    wide[row(0), :] = (conv(1) * conv(2)).T
+    second = pltpu.roll(raw[2], 2, 1)
     fourth = pltpu.roll(raw[0], 4, 1)
-    heads = jnp.where(lane < 2, raw[1], jnp.where(lane < 4, twice[2], fourth))
-    tails = jnp.where(lane < 2, twice[2], jnp.where(lane < 4, fourth, raw[1]))
+    heads = jnp.where(lane < 2, raw[1], jnp.where(lane < 4, second, fourth))
+    tails = jnp.where(lane < 2, second, jnp.where(lane < 4, fourth, raw[1]))
     wide[row(EDGE_ROW), :] = jnp.where(lane < 8, heads, pltpu.roll(tails, 10, 1))
     for copy in filt_loads:
         copy.wait()
@@ -130,22 +132,27 @@
     edge = jnp.concatenate([c, c * flip, d, d * flip], axis=1)
     inner = unfold(waves_ref[half : half + lanes // 2, :])
     w_re, w_im = inner[:, :lanes], inner[:, lanes:]
-    fwd, inv = square(w_re, -w_im, w_im, w_re), square(w_re, w_im, -w_im, w_re)
-    turns = waves_ref[half + lanes // 2 :, :].astype(jnp.float32)
-    cos, sin = turns[:, :size], turns[:, size:]
-
-    part = dot(mixed.astype(jnp.bfloat16), edge, ((1,), (0,)))
-    a_re, a_im = part[:, :size], part[:, size:]
-    b = jnp.concatenate([a_re * cos - a_im * sin, a_re * sin + a_im * cos], axis=0)
-    spec = dot(fwd, b.astype(jnp.bfloat16), ((1,), (0,)))
-    s_re, s_im = spec[:lanes], spec[lanes:]
-    f_re = jnp.concatenate([plane(1), plane(2)], axis=1)
-    f_im = jnp.concatenate([plane(3), plane(4)], axis=1)
-    prod = jnp.concatenate([s_re * f_re - s_im * f_im, s_re * f_im + s_im * f_re], axis=0)
-    time = dot(inv, prod.astype(jnp.bfloat16), ((1,), (0,)))
-    c_re, c_im = time[:lanes], time[lanes:]
-    d = jnp.concatenate([c_re * cos + c_im * sin, c_im * cos - c_re * sin], axis=1)
-    long_out = dot(edge, d.astype(jnp.bfloat16), ((1,), (1,))) * (1.0 / (size * lanes))
+    fwd, inv = square(w_re, w_im, -w_im, w_re), square(w_re, -w_im, w_im, w_re)
+    turns = unfold(waves_ref[2 * half : 4 * half, :]).astype(jnp.float32)
+    cos, sin = turns[:, :lanes], turns[:, lanes:]
+    tall = unfold(waves_ref[4 * half :, :])
+    tall = jnp.concatenate([tall[:, :shards], tall[:, shards:]], axis=0)
+    flip = jnp.where(lane % 2 == 0, 1.0, -1.0).astype(jnp.bfloat16)
+    c, d = tall[:shards], tall[shards:]
+    tall = jnp.concatenate([c, c * flip, d, d * flip], axis=0)
+
+    part = dot(tall, mixed.astype(jnp.bfloat16), ((1,), (1,)))
+    a_re, a_im = part[:size], part[size:]
+    b = jnp.concatenate([a_re * cos - a_im * sin, a_re * sin + a_im * cos], axis=1)
+    spec = dot(b.astype(jnp.bfloat16), fwd, ((1,), (0,)))
+    s_re, s_im = spec[:, :lanes], spec[:, lanes:]
+    f_re = jnp.concatenate([plane(1).T, plane(2).T], axis=0)
+    f_im = jnp.concatenate([plane(3).T, plane(4).T], axis=0)
+    prod = jnp.concatenate([s_re * f_re - s_im * f_im, s_re * f_im + s_im * f_re], axis=1)
+    time = dot(prod.astype(jnp.bfloat16), inv, ((1,), (0,)))
+    c_re, c_im = time[:, :lanes], time[:, lanes:]
+    d = jnp.concatenate([c_re * cos + c_im * sin, c_im * cos - c_re * sin], axis=0)
+    long_out = dot(edge, d.astype(jnp.bfloat16), ((1,), (0,))) * (1.0 / (size * lanes))
     raw = query_ref[...].astype(jnp.float32)
     weight = lambda p: columns_ref[:, p : p + 1]
     gain_ref[...] = jnp.broadcast_to(weight(10), (shards, lanes))

time: 60.2 us -> 60.1 us (level)
  no operation moved by 1% of the time
where the time goes in v8:
time: 60.1 us; the launch traced here: 59.7 us
  blocking collectives  56.7 us (94%)
  Pallas kernels  2.24 us (4%)
  other arithmetic  0.7 us (1%)
    all_to_all x1, blocking collectives, per_device(): lax.all_to_all(sent.reshape(peers, ROWS // 2, 2, tok), 'seq', split_axis=...  31.6 us
    all_to_all x1, blocking collectives, per_device(): lax.all_to_all(part.reshape(peers, 1, tok), 'seq', split_axis=0, concat_a...  17.5 us
    all_gather x1, blocking collectives, per_device(): lax.all_gather(jnp.sum(pre * pre, axis=0)[None], 'tp', axis=0, tiled=True)  7.64 us
    pallas_call x1, Pallas kernels, pack(): pl.pallas_call(pack_kernel, out_shape=(jax.ShapeDtypeStruct((chans * ROWS...  1.38 us

profile of v8, /device:TPU:1, one launch (start us, length us, event | category | flops | bytes accessed | tf_op | source)
XLA Modules:
  0.0 59.7 jit_solution(12278505419194690437)
XLA Ops:
  0.0 0.0 copy-start
  0.0 1.4 %shard_map.64 = (bf16[768,128]{1,0:T(8,128)(2,1)S(1)}, bf16[128,128]{1,0:T(8,128)(2,1)S(1)}, f32[128,16]{1,0:T(8,128)S(1)}, f32[16,128]{1,0:T(8,128)S(1)}) custom-call(bf16[3,128,128]{2,1,0:T(8,128)(2,1)} %proj_hbm.1, f32[2,128,256]{2,1,0:T(8,128)} %filt_hbm.1, f32[3,3,128]{2,1,0:T(4,128)} %bitcast.14, f32[1,128]{1,0:T(1,128)} %bitcast.16, f32[1,128]{1,0:T(1,128)} %bitcast.17), custom_call_target="tpu_custom_call" | custom-call | tf_op jit(solution)/shard_map/pallas_call | solution.py:171
  1.4 31.6 %all_to_all.10 = bf16[128,3,2,128]{3,2,1,0:T(2,128)(2,1)S(1)} all-to-all(bf16[128,3,2,128]{3,2,1,0:T(2,128)(2,1)S(1)} %bitcast.11), channel_id=1, replica_groups=mesh['seq'=128,'tp'=4] {'seq'}, dimensions={0} | all-to-all | bytes 393216 | tf_op jit(solution)/shard_map/all_to_all | solution.py:215
  33.0 0.0 copy-done
  33.0 0.9 %shard_map.65 = (f32[128,128]{1,0:T(8,128)S(1)}, f32[128,128]{1,0:T(8,128)S(1)}, f32[128,128]{1,0:T(8,128)S(1)}) custom-call(bf16[768,128]{1,0:T(8,128)(2,1)S(1)} %bitcast.10, bf16[128,128]{1,0:T(8,128)(2,1)S(1)} %get-tuple-element.13.query_ref, f32[128,16]{1,0:T(8,128)S(1)} %get-tuple-element.14.columns_ref, f32[16,128]{1,0:T(8,128)S(1)} %get-tuple-element.15.own_ref, ...), custom_call_target="tpu_custom_call" | custom-call | tf_op jit(solution)/shard_map/pallas_call | solution.py:198
  33.9 17.5 %all_to_all.11 = f32[128,1,128]{2,1,0:T(1,128)S(1)} all-to-all(f32[128,1,128]{2,1,0:T(1,128)S(1)} %bitcast.12), channel_id=1, replica_groups=mesh['seq'=128,'tp'=4] {'seq'}, dimensions={0} | all-to-all | bytes 131072 | tf_op jit(solution)/shard_map/all_to_all | solution.py:220
  51.4 7.6 %all-gather.1 = f32[4,1,128]{2,1,0:T(1,128)S(1)} all-gather(f32[1,1,128]{2,1,0:T(1,128)S(1)} %bitcast.15), channel_id=2, replica_groups=mesh['seq'=128,'tp'=4] {'tp'}, dimensions={0}, use_global_device_ids=true | all-gather | bytes 2560 | tf_op jit(solution)/shard_map/all_gather | solution.py:224
  59.0 0.6 %multiply_convert_fusion = bf16[128,128]{1,0:T(8,128)(2,1)} fusion(f32[128,128]{1,0:T(8,128)S(1)} %get-tuple-element.18, f32[128,128]{1,0:T(8,128)S(1)} %get-tuple-element.20, f32[128]{0:T(128)S(1)} %add_rsqrt_fusion), kind=kLoop, calls=%fused_computation | loop fusion | flops 49152 | bytes 164352 | tf_op jit(solution)/shard_map/convert_element_type | solution.py:226
  (3 shorter events, 0.1 us)
Async XLA Ops:
  0.0 33.0 %copy-start = (bf16[320,512]{1,0:T(8,128)(2,1)S(1)}, bf16[320,512]{1,0:T(8,128)(2,1)}, u32[]{:S(2)}) copy-start(bf16[320,512]{1,0:T(8,128)(2,1)} %constant.9.clone.waves_ref) | copy-start | bytes 983044

commit v9 on v8

--- a/solution.py
+++ b/solution.py
@@ -64,22 +64,24 @@
     row = lambda r: pl.ds(r, chans, stride=ROWS)
     for copy in proj_loads:
         copy.wait()
-    raw = [proj_ref[i].astype(jnp.float32) for i in range(3)]
+    turned = [proj_ref[i].T.astype(jnp.float32) for i in range(3)]
     place = lax.broadcasted_iota(jnp.int32, (lanes, chans), 0)
 
     def conv(i):
-        x = raw[i].T
+        x = turned[i]
         tap = lambda m: small_ref[3 * i + m : 3 * i + m + 1, :]
         late = tap(1) * jnp.where(place < 1, 0.0, pltpu.roll(x, 1, 0))
         return tap(0) * x + late + tap(2) * jnp.where(place < 2, 0.0, pltpu.roll(x, 2, 0))
 
     query_ref[...] = proj_ref[0]
-    wide[row(0), :] = (conv(1) * conv(2)).T
-    second = pltpu.roll(raw[2], 2, 1)
-    fourth = pltpu.roll(raw[0], 4, 1)
-    heads = jnp.where(lane < 2, raw[1], jnp.where(lane < 4, second, fourth))
-    tails = jnp.where(lane < 2, second, jnp.where(lane < 4, fourth, raw[1]))
-    wide[row(EDGE_ROW), :] = jnp.where(lane < 8, heads, pltpu.roll(tails, 10, 1))
+    wide[row(0), :] = (conv(1) * conv(2)).astype(jnp.bfloat16).T.astype(jnp.float32)
+    at = lax.broadcasted_iota(jnp.int32, (8, chans), 0)
+    q, k, v = ([x[:8], x[lanes - 8 :]] for x in turned)
+    pick = lambda a, b, c: jnp.where(at < 2, a, jnp.where(at < 4, b, c))
+    heads = pick(k[0], pltpu.roll(v[0], 2, 0), pltpu.roll(q[0], 4, 0))
+    tails = pick(pltpu.roll(k[1], 2, 0), pltpu.roll(v[1], 4, 0), pltpu.roll(q[1], 6, 0))
+    edges = jnp.concatenate([heads, tails, jnp.zeros((lanes - 16, chans), jnp.float32)], axis=0)
+    wide[row(EDGE_ROW), :] = edges.astype(jnp.bfloat16).T.astype(jnp.float32)
     for copy in filt_loads:
         copy.wait()
     for part in range(2):
@@ -98,10 +100,11 @@
     size = 2 * shards
     wide[: shards * ROWS, :] = recv_ref[...].astype(jnp.float32)
     plane = lambda r: wide[pl.ds(r, shards, stride=ROWS), :]
+    narrow = lambda r: plane(r).astype(jnp.bfloat16).T.astype(jnp.float32)
     lane = lax.broadcasted_iota(jnp.int32, (shards, lanes), 1)
     shard = lax.broadcasted_iota(jnp.int32, (shards, lanes), 0)
 
-    edges = plane(EDGE_ROW).T
+    edges = narrow(EDGE_ROW)
     at = lax.broadcasted_iota(jnp.int32, (8, shards), 0)
     column = lax.broadcasted_iota(jnp.int32, (8, shards), 1)
     own = lambda p: own_ref[p : p + 1, :]
@@ -111,7 +114,7 @@
     one_ago = jnp.where(at % 2 == 1, pltpu.roll(heads, 1, 0), pltpu.roll(two_ago, 7, 0))
     conv = tap(0) * heads + tap(1) * one_ago + tap(2) * two_ago
     repair = (conv * pltpu.roll(conv, 6, 0)).astype(jnp.bfloat16).astype(jnp.float32)
-    upright = plane(0).T
+    upright = narrow(0)
     mixed = jnp.concatenate([jnp.where(at < 2, repair, upright[:8]), upright[8:]], axis=0)
     rest = jnp.zeros((lanes - 8, shards), jnp.float32)
     spread = lambda x: jnp.concatenate([x, rest], axis=0).T
@@ -146,8 +149,8 @@
     b = jnp.concatenate([a_re * cos - a_im * sin, a_re * sin + a_im * cos], axis=1)
     spec = dot(b.astype(jnp.bfloat16), fwd, ((1,), (0,)))
     s_re, s_im = spec[:, :lanes], spec[:, lanes:]
-    f_re = jnp.concatenate([plane(1).T, plane(2).T], axis=0)
-    f_im = jnp.concatenate([plane(3).T, plane(4).T], axis=0)
+    f_re = jnp.concatenate([narrow(1), narrow(2)], axis=0)
+    f_im = jnp.concatenate([narrow(3), narrow(4)], axis=0)
     prod = jnp.concatenate([s_re * f_re - s_im * f_im, s_re * f_im + s_im * f_re], axis=1)
     time = dot(prod.astype(jnp.bfloat16), inv, ((1,), (0,)))
     c_re, c_im = time[:, :lanes], time[:, lanes:]

time: 60.1 us -> 60 us (level)
  no operation moved by 1% of the time
where the time goes in v9:
time: 60 us; the launch traced here: 59.5 us
  blocking collectives  56.7 us (94%)
  Pallas kernels  2.11 us (4%)
  other arithmetic  0.7 us (1%)
    all_to_all x1, blocking collectives, per_device(): lax.all_to_all(sent.reshape(peers, ROWS // 2, 2, tok), 'seq', split_axis=...  31.6 us
    all_to_all x1, blocking collectives, per_device(): lax.all_to_all(part.reshape(peers, 1, tok), 'seq', split_axis=0, concat_a...  17.5 us
    all_gather x1, blocking collectives, per_device(): lax.all_gather(jnp.sum(pre * pre, axis=0)[None], 'tp', axis=0, tiled=True)  7.64 us
    pallas_call x1, Pallas kernels, pack(): pl.pallas_call(pack_kernel, out_shape=(jax.ShapeDtypeStruct((chans * ROWS...  1.27 us

profile of v9, /device:TPU:1, one launch (start us, length us, event | category | flops | bytes accessed | tf_op | source)
XLA Modules:
  0.0 59.5 jit_solution(4003868677943627404)
XLA Ops:
  0.0 0.0 copy-start
  0.0 1.3 %shard_map.64 = (bf16[768,128]{1,0:T(8,128)(2,1)S(1)}, bf16[128,128]{1,0:T(8,128)(2,1)S(1)}, f32[128,16]{1,0:T(8,128)S(1)}, f32[16,128]{1,0:T(8,128)S(1)}) custom-call(bf16[3,128,128]{2,1,0:T(8,128)(2,1)} %proj_hbm.1, f32[2,128,256]{2,1,0:T(8,128)} %filt_hbm.1, f32[3,3,128]{2,1,0:T(4,128)} %bitcast.14, f32[1,128]{1,0:T(1,128)} %bitcast.16, f32[1,128]{1,0:T(1,128)} %bitcast.17), custom_call_target="tpu_custom_call" | custom-call | tf_op jit(solution)/shard_map/pallas_call | solution.py:174
  1.3 31.6 %all_to_all.10 = bf16[128,3,2,128]{3,2,1,0:T(2,128)(2,1)S(1)} all-to-all(bf16[128,3,2,128]{3,2,1,0:T(2,128)(2,1)S(1)} %bitcast.11), channel_id=1, replica_groups=mesh['seq'=128,'tp'=4] {'seq'}, dimensions={0} | all-to-all | bytes 393216 | tf_op jit(solution)/shard_map/all_to_all | solution.py:218
  32.9 0.0 copy-done
  32.9 0.8 %shard_map.65 = (f32[128,128]{1,0:T(8,128)S(1)}, f32[128,128]{1,0:T(8,128)S(1)}, f32[128,128]{1,0:T(8,128)S(1)}) custom-call(bf16[768,128]{1,0:T(8,128)(2,1)S(1)} %bitcast.10, bf16[128,128]{1,0:T(8,128)(2,1)S(1)} %get-tuple-element.13.query_ref, f32[128,16]{1,0:T(8,128)S(1)} %get-tuple-element.14.columns_ref, f32[16,128]{1,0:T(8,128)S(1)} %get-tuple-element.15.own_ref, ...), custom_call_target="tpu_custom_call" | custom-call | tf_op jit(solution)/shard_map/pallas_call | solution.py:201
  33.7 17.5 %all_to_all.11 = f32[128,1,128]{2,1,0:T(1,128)S(1)} all-to-all(f32[128,1,128]{2,1,0:T(1,128)S(1)} %bitcast.12), channel_id=1, replica_groups=mesh['seq'=128,'tp'=4] {'seq'}, dimensions={0} | all-to-all | bytes 131072 | tf_op jit(solution)/shard_map/all_to_all | solution.py:223
  51.2 7.6 %all-gather.1 = f32[4,1,128]{2,1,0:T(1,128)S(1)} all-gather(f32[1,1,128]{2,1,0:T(1,128)S(1)} %bitcast.15), channel_id=2, replica_groups=mesh['seq'=128,'tp'=4] {'tp'}, dimensions={0}, use_global_device_ids=true | all-gather | bytes 2560 | tf_op jit(solution)/shard_map/all_gather | solution.py:227
  58.9 0.6 %multiply_convert_fusion = bf16[128,128]{1,0:T(8,128)(2,1)} fusion(f32[128,128]{1,0:T(8,128)S(1)} %get-tuple-element.18, f32[128,128]{1,0:T(8,128)S(1)} %get-tuple-element.20, f32[128]{0:T(128)S(1)} %add_rsqrt_fusion), kind=kLoop, calls=%fused_computation | loop fusion | flops 49152 | bytes 164352 | tf_op jit(solution)/shard_map/convert_element_type | solution.py:229
  (3 shorter events, 0.1 us)
Async XLA Ops:
  0.0 32.9 %copy-start = (bf16[320,512]{1,0:T(8,128)(2,1)S(1)}, bf16[320,512]{1,0:T(8,128)(2,1)}, u32[]{:S(2)}) copy-start(bf16[320,512]{1,0:T(8,128)(2,1)} %constant.9.clone.waves_ref) | copy-start | bytes 983044

commit v10 on v9

--- a/solution.py
+++ b/solution.py
@@ -23,7 +23,7 @@
     inner = np.concatenate([np.cos(inner), -np.sin(inner)], axis=1)
     fold = lambda x: np.concatenate([x[: len(x) // 2], x[len(x) // 2 :]], axis=1)
     turns = np.concatenate([np.cos(turn.T), -np.sin(turn.T)], axis=1)
-    rows = [fold(edge), fold(inner), fold(turns), fold(fold(edge.T))]
+    rows = [fold(inner), fold(turns), fold(fold(edge.T))]
     return jnp.asarray(np.concatenate(rows, axis=0), jnp.bfloat16)
 
 
@@ -129,20 +129,17 @@
         a, b, (dims, ((), ())), preferred_element_type=jnp.float32
     )
     half = shards // 2
-    edge = unfold(waves_ref[:half, :])
-    flip = jnp.where(shard % 2 == 0, 1.0, -1.0).astype(jnp.bfloat16)
-    c, d = edge[:, :shards], edge[:, shards:]
-    edge = jnp.concatenate([c, c * flip, d, d * flip], axis=1)
-    inner = unfold(waves_ref[half : half + lanes // 2, :])
+    inner = unfold(waves_ref[: lanes // 2, :])
     w_re, w_im = inner[:, :lanes], inner[:, lanes:]
     fwd, inv = square(w_re, w_im, -w_im, w_re), square(w_re, -w_im, w_im, w_re)
-    turns = unfold(waves_ref[2 * half : 4 * half, :]).astype(jnp.float32)
+    turns = unfold(waves_ref[half : 3 * half, :]).astype(jnp.float32)
     cos, sin = turns[:, :lanes], turns[:, lanes:]
-    tall = unfold(waves_ref[4 * half :, :])
+    tall = unfold(waves_ref[3 * half :, :])
     tall = jnp.concatenate([tall[:, :shards], tall[:, shards:]], axis=0)
     flip = jnp.where(lane % 2 == 0, 1.0, -1.0).astype(jnp.bfloat16)
     c, d = tall[:shards], tall[shards:]
     tall = jnp.concatenate([c, c * flip, d, d * flip], axis=0)
+    edge = tall.T
 
     part = dot(tall, mixed.astype(jnp.bfloat16), ((1,), (1,)))
     a_re, a_im = part[:size], part[size:]

time: 60 us -> 60.1 us (level)
  no operation moved by 1% of the time
where the time goes in v10:
time: 60.1 us; the launch traced here: 59.6 us
  blocking collectives  56.8 us (95%)
  Pallas kernels  2.07 us (3%)
  other arithmetic  0.7 us (1%)
    all_to_all x1, blocking collectives, per_device(): lax.all_to_all(sent.reshape(peers, ROWS // 2, 2, tok), 'seq', split_axis=...  31.7 us
    all_to_all x1, blocking collectives, per_device(): lax.all_to_all(part.reshape(peers, 1, tok), 'seq', split_axis=0, concat_a...  17.5 us
    all_gather x1, blocking collectives, per_device(): lax.all_gather(jnp.sum(pre * pre, axis=0)[None], 'tp', axis=0, tiled=True)  7.64 us
    pallas_call x1, Pallas kernels, pack(): pl.pallas_call(pack_kernel, out_shape=(jax.ShapeDtypeStruct((chans * ROWS...  1.22 us

profile of v10, /device:TPU:1, one launch (start us, length us, event | category | flops | bytes accessed | tf_op | source)
XLA Modules:
  0.0 59.6 jit_solution(11420111835404824323)
XLA Ops:
  0.0 1.2 %shard_map.64 = (bf16[768,128]{1,0:T(8,128)(2,1)S(1)}, bf16[128,128]{1,0:T(8,128)(2,1)S(1)}, f32[128,16]{1,0:T(8,128)S(1)}, f32[16,128]{1,0:T(8,128)S(1)}) custom-call(bf16[3,128,128]{2,1,0:T(8,128)(2,1)} %proj_hbm.1, f32[2,128,256]{2,1,0:T(8,128)} %filt_hbm.1, f32[3,3,128]{2,1,0:T(4,128)} %bitcast.14, f32[1,128]{1,0:T(1,128)} %bitcast.16, f32[1,128]{1,0:T(1,128)} %bitcast.17), custom_call_target="tpu_custom_call" | custom-call | tf_op jit(solution)/shard_map/pallas_call | solution.py:171
  1.2 0.0 copy-start
  1.2 31.7 %all_to_all.10 = bf16[128,3,2,128]{3,2,1,0:T(2,128)(2,1)S(1)} all-to-all(bf16[128,3,2,128]{3,2,1,0:T(2,128)(2,1)S(1)} %bitcast.11), channel_id=1, replica_groups=mesh['seq'=128,'tp'=4] {'seq'}, dimensions={0} | all-to-all | bytes 393216 | tf_op jit(solution)/shard_map/all_to_all | solution.py:215
  33.0 0.0 copy-done
  33.0 0.8 %shard_map.65 = (f32[128,128]{1,0:T(8,128)S(1)}, f32[128,128]{1,0:T(8,128)S(1)}, f32[128,128]{1,0:T(8,128)S(1)}) custom-call(bf16[768,128]{1,0:T(8,128)(2,1)S(1)} %bitcast.10, bf16[128,128]{1,0:T(8,128)(2,1)S(1)} %get-tuple-element.13.query_ref, f32[128,16]{1,0:T(8,128)S(1)} %get-tuple-element.14.columns_ref, f32[16,128]{1,0:T(8,128)S(1)} %get-tuple-element.15.own_ref, ...), custom_call_target="tpu_custom_call" | custom-call | tf_op jit(solution)/shard_map/pallas_call | solution.py:198
  33.8 17.5 %all_to_all.11 = f32[128,1,128]{2,1,0:T(1,128)S(1)} all-to-all(f32[128,1,128]{2,1,0:T(1,128)S(1)} %bitcast.12), channel_id=1, replica_groups=mesh['seq'=128,'tp'=4] {'seq'}, dimensions={0} | all-to-all | bytes 131072 | tf_op jit(solution)/shard_map/all_to_all | solution.py:220
  51.3 7.6 %all-gather.1 = f32[4,1,128]{2,1,0:T(1,128)S(1)} all-gather(f32[1,1,128]{2,1,0:T(1,128)S(1)} %bitcast.15), channel_id=2, replica_groups=mesh['seq'=128,'tp'=4] {'tp'}, dimensions={0}, use_global_device_ids=true | all-gather | bytes 2560 | tf_op jit(solution)/shard_map/all_gather | solution.py:224
  59.0 0.6 %multiply_convert_fusion = bf16[128,128]{1,0:T(8,128)(2,1)} fusion(f32[128,128]{1,0:T(8,128)S(1)} %get-tuple-element.18, f32[128,128]{1,0:T(8,128)S(1)} %get-tuple-element.20, f32[128]{0:T(128)S(1)} %add_rsqrt_fusion), kind=kLoop, calls=%fused_computation | loop fusion | flops 49152 | bytes 164352 | tf_op jit(solution)/shard_map/convert_element_type | solution.py:226
  (3 shorter events, 0.1 us)
Async XLA Ops:
  1.2 31.7 %copy-start = (bf16[256,512]{1,0:T(8,128)(2,1)S(1)}, bf16[256,512]{1,0:T(8,128)(2,1)}, u32[]{:S(2)}) copy-start(bf16[256,512]{1,0:T(8,128)(2,1)} %constant.9.clone.waves_ref) | copy-start | bytes 786436

commit v11 on v10

--- a/solution.py
+++ b/solution.py
@@ -221,8 +221,9 @@
         part.reshape(peers, 1, tok), "seq", split_axis=0, concat_axis=0, tiled=True
     )
     pre = part.reshape(chans, tok) * factor
-    squares = lax.all_gather(jnp.sum(pre * pre, axis=0)[None], "tp", axis=0, tiled=True)
-    meansq = jnp.sum(squares, axis=0) / (chans * groups)
+    squares = jnp.broadcast_to(jnp.sum(pre * pre, axis=0)[None, None], (groups, 1, tok))
+    squares = lax.all_to_all(squares, "tp", split_axis=0, concat_axis=0, tiled=True)
+    meansq = jnp.sum(squares[:, 0], axis=0) / (chans * groups)
     return (pre * lax.rsqrt(meansq + 1e-05)[None, :] * gain).astype(jnp.bfloat16)
 
 

time: 60.1 us -> 60.1 us (level)
    all_to_all x0 -> x1, blocking collectives: none -> 7.92 us  [per_device(): lax.all_to_all(squares, 'tp', split_axis=0, concat_axis=0, tiled=True)]
    all_gather x1 -> x0, blocking collectives: 7.64 us -> none  [per_device(): lax.all_gather(jnp.sum(pre * pre, axis=0)[None], 'tp', axis=0, tiled=True)]
where the time goes in v11:
time: 60.1 us; the launch traced here: 59.9 us
  blocking collectives  57.1 us (95%)
  Pallas kernels  2.07 us (3%)
  other arithmetic  0.7 us (1%)
    all_to_all x1, blocking collectives, per_device(): lax.all_to_all(sent.reshape(peers, ROWS // 2, 2, tok), 'seq', split_axis=...  31.7 us
    all_to_all x1, blocking collectives, per_device(): lax.all_to_all(part.reshape(peers, 1, tok), 'seq', split_axis=0, concat_a...  17.5 us
    all_to_all x1, blocking collectives, per_device(): lax.all_to_all(squares, 'tp', split_axis=0, concat_axis=0, tiled=True)  7.92 us
    pallas_call x1, Pallas kernels, pack(): pl.pallas_call(pack_kernel, out_shape=(jax.ShapeDtypeStruct((chans * ROWS...  1.22 us

profile of v11, /device:TPU:1, one launch (start us, length us, event | category | flops | bytes accessed | tf_op | source)
XLA Modules:
  0.0 59.9 jit_solution(16026892431152021710)
XLA Ops:
  0.0 1.2 %shard_map.64 = (bf16[768,128]{1,0:T(8,128)(2,1)S(1)}, bf16[128,128]{1,0:T(8,128)(2,1)S(1)}, f32[128,16]{1,0:T(8,128)S(1)}, f32[16,128]{1,0:T(8,128)S(1)}) custom-call(bf16[3,128,128]{2,1,0:T(8,128)(2,1)} %proj_hbm.1, f32[2,128,256]{2,1,0:T(8,128)} %filt_hbm.1, f32[3,3,128]{2,1,0:T(4,128)} %bitcast.15, f32[1,128]{1,0:T(1,128)} %bitcast.16, f32[1,128]{1,0:T(1,128)} %bitcast.17), custom_call_target="tpu_custom_call" | custom-call | tf_op jit(solution)/shard_map/pallas_call | solution.py:171
  1.2 0.0 copy-start
  1.2 31.7 %all_to_all.15 = bf16[128,3,2,128]{3,2,1,0:T(2,128)(2,1)S(1)} all-to-all(bf16[128,3,2,128]{3,2,1,0:T(2,128)(2,1)S(1)} %bitcast.11), channel_id=1, replica_groups=mesh['seq'=128,'tp'=4] {'seq'}, dimensions={0} | all-to-all | bytes 393216 | tf_op jit(solution)/shard_map/all_to_all | solution.py:215
  33.0 0.0 copy-done
  33.0 0.8 %shard_map.65 = (f32[128,128]{1,0:T(8,128)S(1)}, f32[128,128]{1,0:T(8,128)S(1)}, f32[128,128]{1,0:T(8,128)S(1)}) custom-call(bf16[768,128]{1,0:T(8,128)(2,1)S(1)} %bitcast.10, bf16[128,128]{1,0:T(8,128)(2,1)S(1)} %get-tuple-element.13.query_ref, f32[128,16]{1,0:T(8,128)S(1)} %get-tuple-element.14.columns_ref, f32[16,128]{1,0:T(8,128)S(1)} %get-tuple-element.15.own_ref, ...), custom_call_target="tpu_custom_call" | custom-call | tf_op jit(solution)/shard_map/pallas_call | solution.py:198
  33.8 17.5 %all_to_all.16 = f32[128,1,128]{2,1,0:T(1,128)S(1)} all-to-all(f32[128,1,128]{2,1,0:T(1,128)S(1)} %bitcast.12), channel_id=1, replica_groups=mesh['seq'=128,'tp'=4] {'seq'}, dimensions={0} | all-to-all | bytes 131072 | tf_op jit(solution)/shard_map/all_to_all | solution.py:220
  51.3 7.9 %all_to_all.17 = f32[4,1,128]{2,1,0:T(1,128)S(1)} all-to-all(f32[4,1,128]{2,1,0:T(1,128)S(1)} %broadcast_in_dim.15), channel_id=1, replica_groups=mesh['seq'=128,'tp'=4] {'tp'}, dimensions={0} | all-to-all | bytes 4096 | tf_op jit(solution)/shard_map/all_to_all | solution.py:225
  59.3 0.6 %multiply_convert_fusion = bf16[128,128]{1,0:T(8,128)(2,1)} fusion(f32[128,128]{1,0:T(8,128)S(1)} %get-tuple-element.18, f32[128,128]{1,0:T(8,128)S(1)} %get-tuple-element.20, f32[128]{0:T(128)S(1)} %add_rsqrt_fusion), kind=kLoop, calls=%fused_computation | loop fusion | flops 49152 | bytes 164352 | tf_op jit(solution)/shard_map/convert_element_type | solution.py:227
  (4 shorter events, 0.1 us)
Async XLA Ops:
  1.2 31.7 %copy-start = (bf16[256,512]{1,0:T(8,128)(2,1)S(1)}, bf16[256,512]{1,0:T(8,128)(2,1)}, u32[]{:S(2)}) copy-start(bf16[256,512]{1,0:T(8,128)(2,1)} %constant.9.clone.waves_ref) | copy-start | bytes 786436

commit v12 on v11

--- a/solution.py
+++ b/solution.py
@@ -80,7 +80,11 @@
     pick = lambda a, b, c: jnp.where(at < 2, a, jnp.where(at < 4, b, c))
     heads = pick(k[0], pltpu.roll(v[0], 2, 0), pltpu.roll(q[0], 4, 0))
     tails = pick(pltpu.roll(k[1], 2, 0), pltpu.roll(v[1], 4, 0), pltpu.roll(q[1], 6, 0))
-    edges = jnp.concatenate([heads, tails, jnp.zeros((lanes - 16, chans), jnp.float32)], axis=0)
+    odd = at % 2 == 1
+    own_ago = jnp.where(odd, pltpu.roll(heads, 1, 0), 0.0)
+    past_ago = jnp.where(odd, 0.0, pltpu.roll(tails, 7, 0))
+    spare = jnp.zeros((lanes - 32, chans), jnp.float32)
+    edges = jnp.concatenate([heads, tails, own_ago, past_ago, spare], axis=0)
     wide[row(EDGE_ROW), :] = edges.astype(jnp.bfloat16).T.astype(jnp.float32)
     for copy in filt_loads:
         copy.wait()
@@ -111,7 +115,8 @@
     tap = lambda m: jnp.where(at < 2, own(3 + m), jnp.where(at < 4, own(6 + m), own(m)))
     heads = edges[:8]
     two_ago = jnp.where(column == 0, 0.0, pltpu.roll(edges[8:16], 1, 1))
-    one_ago = jnp.where(at % 2 == 1, pltpu.roll(heads, 1, 0), pltpu.roll(two_ago, 7, 0))
+    past_ago = jnp.where(column == 0, 0.0, pltpu.roll(edges[24:32], 1, 1))
+    one_ago = edges[16:24] + past_ago
     conv = tap(0) * heads + tap(1) * one_ago + tap(2) * two_ago
     repair = (conv * pltpu.roll(conv, 6, 0)).astype(jnp.bfloat16).astype(jnp.float32)
     upright = narrow(0)

time: 60.1 us -> 60.1 us (level)
  no operation moved by 1% of the time
where the time goes in v12:
time: 60.1 us; the launch traced here: 59.9 us
  blocking collectives  57.1 us (95%)
  Pallas kernels  2.07 us (3%)
  other arithmetic  0.7 us (1%)
    all_to_all x1, blocking collectives, per_device(): lax.all_to_all(sent.reshape(peers, ROWS // 2, 2, tok), 'seq', split_axis=...  31.7 us
    all_to_all x1, blocking collectives, per_device(): lax.all_to_all(part.reshape(peers, 1, tok), 'seq', split_axis=0, concat_a...  17.5 us
    all_to_all x1, blocking collectives, per_device(): lax.all_to_all(squares, 'tp', split_axis=0, concat_axis=0, tiled=True)  7.91 us
    pallas_call x1, Pallas kernels, pack(): pl.pallas_call(pack_kernel, out_shape=(jax.ShapeDtypeStruct((chans * ROWS...  1.22 us

profile of v12, /device:TPU:1, one launch (start us, length us, event | category | flops | bytes accessed | tf_op | source)
XLA Modules:
  0.0 59.9 jit_solution(6181959922681267726)
XLA Ops:
  0.0 1.2 %shard_map.64 = (bf16[768,128]{1,0:T(8,128)(2,1)S(1)}, bf16[128,128]{1,0:T(8,128)(2,1)S(1)}, f32[128,16]{1,0:T(8,128)S(1)}, f32[16,128]{1,0:T(8,128)S(1)}) custom-call(bf16[3,128,128]{2,1,0:T(8,128)(2,1)} %proj_hbm.1, f32[2,128,256]{2,1,0:T(8,128)} %filt_hbm.1, f32[3,3,128]{2,1,0:T(4,128)} %bitcast.15, f32[1,128]{1,0:T(1,128)} %bitcast.16, f32[1,128]{1,0:T(1,128)} %bitcast.17), custom_call_target="tpu_custom_call" | custom-call | tf_op jit(solution)/shard_map/pallas_call | solution.py:176
  1.2 0.0 copy-start
  1.2 31.7 %all_to_all.15 = bf16[128,3,2,128]{3,2,1,0:T(2,128)(2,1)S(1)} all-to-all(bf16[128,3,2,128]{3,2,1,0:T(2,128)(2,1)S(1)} %bitcast.11), channel_id=1, replica_groups=mesh['seq'=128,'tp'=4] {'seq'}, dimensions={0} | all-to-all | bytes 393216 | tf_op jit(solution)/shard_map/all_to_all | solution.py:220
  33.0 0.0 copy-done
  33.0 0.8 %shard_map.65 = (f32[128,128]{1,0:T(8,128)S(1)}, f32[128,128]{1,0:T(8,128)S(1)}, f32[128,128]{1,0:T(8,128)S(1)}) custom-call(bf16[768,128]{1,0:T(8,128)(2,1)S(1)} %bitcast.10, bf16[128,128]{1,0:T(8,128)(2,1)S(1)} %get-tuple-element.13.query_ref, f32[128,16]{1,0:T(8,128)S(1)} %get-tuple-element.14.columns_ref, f32[16,128]{1,0:T(8,128)S(1)} %get-tuple-element.15.own_ref, ...), custom_call_target="tpu_custom_call" | custom-call | tf_op jit(solution)/shard_map/pallas_call | solution.py:203
  33.8 17.5 %all_to_all.16 = f32[128,1,128]{2,1,0:T(1,128)S(1)} all-to-all(f32[128,1,128]{2,1,0:T(1,128)S(1)} %bitcast.12), channel_id=1, replica_groups=mesh['seq'=128,'tp'=4] {'seq'}, dimensions={0} | all-to-all | bytes 131072 | tf_op jit(solution)/shard_map/all_to_all | solution.py:225
  51.3 7.9 %all_to_all.17 = f32[4,1,128]{2,1,0:T(1,128)S(1)} all-to-all(f32[4,1,128]{2,1,0:T(1,128)S(1)} %broadcast_in_dim.15), channel_id=1, replica_groups=mesh['seq'=128,'tp'=4] {'tp'}, dimensions={0} | all-to-all | bytes 4096 | tf_op jit(solution)/shard_map/all_to_all | solution.py:230
  59.3 0.6 %multiply_convert_fusion = bf16[128,128]{1,0:T(8,128)(2,1)} fusion(f32[128,128]{1,0:T(8,128)S(1)} %get-tuple-element.18, f32[128,128]{1,0:T(8,128)S(1)} %get-tuple-element.20, f32[128]{0:T(128)S(1)} %add_rsqrt_fusion), kind=kLoop, calls=%fused_computation | loop fusion | flops 49152 | bytes 164352 | tf_op jit(solution)/shard_map/convert_element_type | solution.py:232
  (4 shorter events, 0.1 us)
Async XLA Ops:
  1.2 31.7 %copy-start = (bf16[256,512]{1,0:T(8,128)(2,1)S(1)}, bf16[256,512]{1,0:T(8,128)(2,1)}, u32[]{:S(2)}) copy-start(bf16[256,512]{1,0:T(8,128)(2,1)} %constant.9.clone.waves_ref) | copy-start | bytes 786436

commit v13 on v11

--- a/solution.py
+++ b/solution.py
@@ -131,7 +131,10 @@
     half = shards // 2
     inner = unfold(waves_ref[: lanes // 2, :])
     w_re, w_im = inner[:, :lanes], inner[:, lanes:]
-    fwd, inv = square(w_re, w_im, -w_im, w_re), square(w_re, -w_im, w_im, w_re)
+    fwd = square(w_re, w_im, -w_im, w_re)
+    scale = jnp.asarray(1.0 / (size * lanes), jnp.bfloat16)
+    w_re, w_im = w_re * scale, w_im * scale
+    inv = square(w_re, -w_im, w_im, w_re)
     turns = unfold(waves_ref[half : 3 * half, :]).astype(jnp.float32)
     cos, sin = turns[:, :lanes], turns[:, lanes:]
     tall = unfold(waves_ref[3 * half :, :])
@@ -152,7 +155,7 @@
     time = dot(prod.astype(jnp.bfloat16), inv, ((1,), (0,)))
     c_re, c_im = time[:, :lanes], time[:, lanes:]
     d = jnp.concatenate([c_re * cos + c_im * sin, c_im * cos - c_re * sin], axis=0)
-    long_out = dot(edge, d.astype(jnp.bfloat16), ((1,), (0,))) * (1.0 / (size * lanes))
+    long_out = dot(edge, d.astype(jnp.bfloat16), ((1,), (0,)))
     raw = query_ref[...].astype(jnp.float32)
     weight = lambda p: columns_ref[:, p : p + 1]
     gain_ref[...] = jnp.broadcast_to(weight(10), (shards, lanes))

time: 60.1 us -> 60.1 us (level)
  no operation moved by 1% of the time
where the time goes in v13:
time: 60.1 us; the launch traced here: 59.9 us
  blocking collectives  57.1 us (95%)
  Pallas kernels  2.06 us (3%)
  other arithmetic  0.7 us (1%)
    all_to_all x1, blocking collectives, per_device(): lax.all_to_all(sent.reshape(peers, ROWS // 2, 2, tok), 'seq', split_axis=...  31.7 us
    all_to_all x1, blocking collectives, per_device(): lax.all_to_all(part.reshape(peers, 1, tok), 'seq', split_axis=0, concat_a...  17.5 us
    all_to_all x1, blocking collectives, per_device(): lax.all_to_all(squares, 'tp', split_axis=0, concat_axis=0, tiled=True)  7.91 us
    pallas_call x1, Pallas kernels, pack(): pl.pallas_call(pack_kernel, out_shape=(jax.ShapeDtypeStruct((chans * ROWS...  1.22 us

profile of v13, /device:TPU:1, one launch (start us, length us, event | category | flops | bytes accessed | tf_op | source)
XLA Modules:
  0.0 59.9 jit_solution(10603030169944277360)
XLA Ops:
  0.0 1.2 %shard_map.64 = (bf16[768,128]{1,0:T(8,128)(2,1)S(1)}, bf16[128,128]{1,0:T(8,128)(2,1)S(1)}, f32[128,16]{1,0:T(8,128)S(1)}, f32[16,128]{1,0:T(8,128)S(1)}) custom-call(bf16[3,128,128]{2,1,0:T(8,128)(2,1)} %proj_hbm.1, f32[2,128,256]{2,1,0:T(8,128)} %filt_hbm.1, f32[3,3,128]{2,1,0:T(4,128)} %bitcast.15, f32[1,128]{1,0:T(1,128)} %bitcast.16, f32[1,128]{1,0:T(1,128)} %bitcast.17), custom_call_target="tpu_custom_call" | custom-call | tf_op jit(solution)/shard_map/pallas_call | solution.py:174
  1.2 0.0 copy-start
  1.2 31.7 %all_to_all.15 = bf16[128,3,2,128]{3,2,1,0:T(2,128)(2,1)S(1)} all-to-all(bf16[128,3,2,128]{3,2,1,0:T(2,128)(2,1)S(1)} %bitcast.11), channel_id=1, replica_groups=mesh['seq'=128,'tp'=4] {'seq'}, dimensions={0} | all-to-all | bytes 393216 | tf_op jit(solution)/shard_map/all_to_all | solution.py:218
  33.0 0.0 copy-done
  33.0 0.8 %shard_map.65 = (f32[128,128]{1,0:T(8,128)S(1)}, f32[128,128]{1,0:T(8,128)S(1)}, f32[128,128]{1,0:T(8,128)S(1)}) custom-call(bf16[768,128]{1,0:T(8,128)(2,1)S(1)} %bitcast.10, bf16[128,128]{1,0:T(8,128)(2,1)S(1)} %get-tuple-element.13.query_ref, f32[128,16]{1,0:T(8,128)S(1)} %get-tuple-element.14.columns_ref, f32[16,128]{1,0:T(8,128)S(1)} %get-tuple-element.15.own_ref, ...), custom_call_target="tpu_custom_call" | custom-call | tf_op jit(solution)/shard_map/pallas_call | solution.py:201
  33.8 17.5 %all_to_all.16 = f32[128,1,128]{2,1,0:T(1,128)S(1)} all-to-all(f32[128,1,128]{2,1,0:T(1,128)S(1)} %bitcast.12), channel_id=1, replica_groups=mesh['seq'=128,'tp'=4] {'seq'}, dimensions={0} | all-to-all | bytes 131072 | tf_op jit(solution)/shard_map/all_to_all | solution.py:223
  51.3 7.9 %all_to_all.17 = f32[4,1,128]{2,1,0:T(1,128)S(1)} all-to-all(f32[4,1,128]{2,1,0:T(1,128)S(1)} %broadcast_in_dim.15), channel_id=1, replica_groups=mesh['seq'=128,'tp'=4] {'tp'}, dimensions={0} | all-to-all | bytes 4096 | tf_op jit(solution)/shard_map/all_to_all | solution.py:228
  59.3 0.6 %multiply_convert_fusion = bf16[128,128]{1,0:T(8,128)(2,1)} fusion(f32[128,128]{1,0:T(8,128)S(1)} %get-tuple-element.18, f32[128,128]{1,0:T(8,128)S(1)} %get-tuple-element.20, f32[128]{0:T(128)S(1)} %add_rsqrt_fusion), kind=kLoop, calls=%fused_computation | loop fusion | flops 49152 | bytes 164352 | tf_op jit(solution)/shard_map/convert_element_type | solution.py:230
  (4 shorter events, 0.1 us)
Async XLA Ops:
  1.2 31.7 %copy-start = (bf16[256,512]{1,0:T(8,128)(2,1)S(1)}, bf16[256,512]{1,0:T(8,128)(2,1)}, u32[]{:S(2)}) copy-start(bf16[256,512]{1,0:T(8,128)(2,1)} %constant.9.clone.waves_ref) | copy-start | bytes 786436
